TPU v7x, 256 devices: a whole 4x4x8 slice. The times are simulated.
256 devices in a mesh: tm: 8 (over x, core), port: 32 (over y, z).
Axes of the slice: x: 4, y: 4, z: 8, core: 2. Of those that a mesh axis runs over, the one named last changes fastest.
Arguments:
- counters: bfloat16 [8192, 256], P('tm'), may hold values from -6 to 6
- signatures: bfloat16 [256, 8192], P(None, 'port'), may hold values from -0.375 to 0.375
- eigen_vectors_at_pins: bfloat16 [8192, 256], P('port'), may hold values from -0.125 to 0.125
- taps: bfloat16 [256, 4096], P('port'), may hold values from -0.5 to 0.5
Outputs:
- voltage_sag: bfloat16 [8192, 8192], P('tm', 'port')
All inputs are finite; a program needn't handle non-finite values.
Results may differ from a plain program's by a relative error of at most 0.007.
Values may be sent and summed in bfloat16 or wider, within the bound.
No kernel may reach another device: no remote copies, remote signals or barrier semaphores. Data moves between devices by JAX's collectives and lax.ppermute only.
A program may use at most 128 MiB of HBM per device.

v0:
```python
import jax
import jax.numpy as jnp
from jax import lax
from jax.sharding import PartitionSpec as P


def passed_along(value, axis, steps):
    count = lax.axis_size(axis)
    initial, last = (max(0, -steps), min(count, count - steps))
    return lax.ppermute(value, axis, [(source, source + steps) for source in range(initial, last)])


def banded_convolution_tile(local_taps, lag, width):
    own = local_taps.shape[0]
    padded = jnp.concatenate(
        [
            jnp.zeros((own, width), local_taps.dtype),
            local_taps,
            jnp.zeros((own, 2 * width), local_taps.dtype),
        ],
        axis=1,
    )
    start = lag * width + 1
    segment = padded[:, start : start + 2 * width]
    tiled = jnp.tile(segment, (1, width + 1))
    skewed = tiled[:, : width * (2 * width + 1)].reshape(own, width, 2 * width + 1)
    return jnp.flip(skewed[:, :, :width], axis=2)


def convolve(local_taps, blocks, lags, count, width):
    total = jnp.zeros((blocks.shape[0], count, width), jnp.float32)
    for lag in range(lags + 1):
        coupling_matrix = banded_convolution_tile(local_taps, lag, width)
        source_signal = blocks[:, lags - lag : lags - lag + count, :]
        total = total + jnp.einsum(
            "nds,nxs->nxd", coupling_matrix, source_signal, preferred_element_type=jnp.float32
        )
    return total.reshape(blocks.shape[0], count * width)


def per_device(counters, signatures, eigen_vectors_at_pins, taps):
    own_modes = taps.shape[0]
    span = taps.shape[1]
    cycle_span = counters.shape[0]
    width = min(256, cycle_span)
    lags = (span - 2) // width + 1
    nblocks = cycle_span // width
    currents = jnp.dot(counters, signatures, preferred_element_type=jnp.float32)
    modes_wide = eigen_vectors_at_pins.astype(jnp.float32)
    projected = lax.psum_scatter(
        jnp.einsum("pm,tp->mt", modes_wide, currents, precision=lax.Precision.HIGHEST),
        "port",
        scatter_dimension=0,
        tiled=True,
    )
    modal = projected.astype(jnp.bfloat16)
    reach = (span - 2) // cycle_span + 1
    preceding_terms = []
    for back in range(reach, 0, -1):
        preceding_terms.append(passed_along(modal, "tm", back))
    prefix = jnp.concatenate(preceding_terms, axis=1)
    extended = jnp.concatenate([prefix, modal], axis=1)
    blocks = extended.reshape(own_modes, lags + nblocks, width)
    kernel_taps_per_mode = convolve(taps, blocks, lags, nblocks, width)
    kernel_taps_per_mode = kernel_taps_per_mode.astype(jnp.bfloat16)
    complete_interval = lax.all_gather(kernel_taps_per_mode, "port", axis=0, tiled=True)
    voltage_sag = jnp.einsum(
        "vm,uv->mu", complete_interval, eigen_vectors_at_pins, preferred_element_type=jnp.float32
    )
    return voltage_sag.astype(jnp.bfloat16)


def solution(mesh):
    in_specs = (P("tm", None), P(None, "port"), P("port", None), P("port", None))
    out_specs = P("tm", "port")
    return jax.shard_map(
        per_device, mesh=mesh, in_specs=in_specs, out_specs=out_specs, check_vma=False
    )
```

profile of v0, /device:TPU:32, one launch (start us, length us, event | category | flops | bytes accessed | tf_op | source)
XLA Modules:
  0.0 715.0 jit_solution(13024404569382758246)
XLA Ops:
  11.7 216.2 %reduce-scatter.4.cloned.1.call-done = f32[8,1024]{1,0:T(8,128)} async-done(((f32[256,1024]{1,0:T(8,128)}), f32[8,1024]{1,0:T(8,128)}) %reduce-scatter.4.cloned.1.call-update) | async-done | bytes 32784
  239.3 6.6 reshape.125
  263.1 11.3 %rev.53 = bf16[8,256,256]{2,1,0:T(8,128)(2,1)} reverse(bf16[8,256,256]{2,1,0:T(8,128)(2,1)S(1)} %slice-done.1), dimensions={2} | reverse | bytes 2097152 | tf_op jit(solution)/shard_map/jit(_flip)/rev | solution.py:27
  287.3 11.3 %rev.54 = bf16[8,256,256]{2,1,0:T(8,128)(2,1)} reverse(bf16[8,256,256]{2,1,0:T(8,128)(2,1)S(1)} %slice-done.2), dimensions={2} | reverse | bytes 2097152 | tf_op jit(solution)/shard_map/jit(_flip)/rev | solution.py:27
  303.3 6.6 reshape.128
  311.2 11.3 %rev.55 = bf16[8,256,256]{2,1,0:T(8,128)(2,1)} reverse(bf16[8,256,256]{2,1,0:T(8,128)(2,1)S(1)} %slice-done.3), dimensions={2} | reverse | bytes 2097152 | tf_op jit(solution)/shard_map/jit(_flip)/rev | solution.py:27
  335.6 11.3 %rev.56 = bf16[8,256,256]{2,1,0:T(8,128)(2,1)} reverse(bf16[8,256,256]{2,1,0:T(8,128)(2,1)S(1)} %slice-done.4), dimensions={2} | reverse | bytes 2097152 | tf_op jit(solution)/shard_map/jit(_flip)/rev | solution.py:27
  359.6 11.3 %rev.57 = bf16[8,256,256]{2,1,0:T(8,128)(2,1)} reverse(bf16[8,256,256]{2,1,0:T(8,128)(2,1)S(1)} %slice-done.5), dimensions={2} | reverse | bytes 2097152 | tf_op jit(solution)/shard_map/jit(_flip)/rev | solution.py:27
  375.8 6.7 reshape.131
  383.8 11.3 %rev.58 = bf16[8,256,256]{2,1,0:T(8,128)(2,1)} reverse(bf16[8,256,256]{2,1,0:T(8,128)(2,1)S(1)} %slice-done.6), dimensions={2} | reverse | bytes 2097152 | tf_op jit(solution)/shard_map/jit(_flip)/rev | solution.py:27
  399.9 6.7 reshape.132
  407.7 11.3 %rev.59 = bf16[8,256,256]{2,1,0:T(8,128)(2,1)} reverse(bf16[8,256,256]{2,1,0:T(8,128)(2,1)S(1)} %slice-done.7), dimensions={2} | reverse | bytes 2097152 | tf_op jit(solution)/shard_map/jit(_flip)/rev | solution.py:27
  431.9 11.3 %rev.60 = bf16[8,256,256]{2,1,0:T(8,128)(2,1)} reverse(bf16[8,256,256]{2,1,0:T(8,128)(2,1)S(1)} %slice-done.8), dimensions={2} | reverse | bytes 2097152 | tf_op jit(solution)/shard_map/jit(_flip)/rev | solution.py:27
  455.9 11.3 %rev.61 = bf16[8,256,256]{2,1,0:T(8,128)(2,1)} reverse(bf16[8,256,256]{2,1,0:T(8,128)(2,1)S(1)} %slice-done.9), dimensions={2} | reverse | bytes 2097152 | tf_op jit(solution)/shard_map/jit(_flip)/rev | solution.py:27
  472.4 6.7 reshape.135
  480.2 11.2 %rev.62 = bf16[8,256,256]{2,1,0:T(8,128)(2,1)} reverse(bf16[8,256,256]{2,1,0:T(8,128)(2,1)S(1)} %slice-done.10), dimensions={2} | reverse | bytes 2097152 | tf_op jit(solution)/shard_map/jit(_flip)/rev | solution.py:27
  504.1 11.3 %rev.63 = bf16[8,256,256]{2,1,0:T(8,128)(2,1)} reverse(bf16[8,256,256]{2,1,0:T(8,128)(2,1)S(1)} %slice-done.11), dimensions={2} | reverse | bytes 2097152 | tf_op jit(solution)/shard_map/jit(_flip)/rev | solution.py:27
  528.2 11.3 %rev.64 = bf16[8,256,256]{2,1,0:T(8,128)(2,1)} reverse(bf16[8,256,256]{2,1,0:T(8,128)(2,1)S(1)} %slice-done.12), dimensions={2} | reverse | bytes 2097152 | tf_op jit(solution)/shard_map/jit(_flip)/rev | solution.py:27
  544.3 6.6 reshape.138
  552.2 11.3 %rev.65 = bf16[8,256,256]{2,1,0:T(8,128)(2,1)} reverse(bf16[8,256,256]{2,1,0:T(8,128)(2,1)S(1)} %slice-done.13), dimensions={2} | reverse | bytes 2097152 | tf_op jit(solution)/shard_map/jit(_flip)/rev | solution.py:27
  576.3 11.3 %rev.66 = bf16[8,256,256]{2,1,0:T(8,128)(2,1)} reverse(bf16[8,256,256]{2,1,0:T(8,128)(2,1)S(1)} %slice-done.14), dimensions={2} | reverse | bytes 2097152 | tf_op jit(solution)/shard_map/jit(_flip)/rev | solution.py:27
  600.3 11.3 %rev.67 = bf16[8,256,256]{2,1,0:T(8,128)(2,1)} reverse(bf16[8,256,256]{2,1,0:T(8,128)(2,1)S(1)} %slice-done.15), dimensions={2} | reverse | bytes 2097152 | tf_op jit(solution)/shard_map/jit(_flip)/rev | solution.py:27
  624.4 11.2 %rev.68 = bf16[8,256,256]{2,1,0:T(8,128)(2,1)} reverse(bf16[8,256,256]{2,1,0:T(8,128)(2,1)S(1)} %slice-done.16), dimensions={2} | reverse | bytes 2097152 | tf_op jit(solution)/shard_map/jit(_flip)/rev | solution.py:27
  658.3 48.2 %all_gather.3 = bf16[256,1024]{1,0:T(8,128)(2,1)S(1)} all-gather(bf16[8,1024]{1,0:T(8,128)(2,1)S(1)} %bitcast.65), channel_id=1, replica_groups=mesh['tm'=8,'port'=32] {'port'}, dimensions={0}, use_global_device_ids=true | all-gather | bytes 540672 | tf_op jit(solution)/shard_map/all_gather | solution.py:66
  (182 shorter events, 216.0 us)
Async XLA Ops:
  6.5 221.3 %reduce-scatter.4.cloned.1.call-start = ((), (), s32[]{:S(2)}) async-start(), calls=%async_computation.1 | async-start | bytes 1081344
  10.3 224.1 %copy-start.19 = (bf16[8,4096]{1,0:T(8,128)(2,1)S(1)}, bf16[8,4096]{1,0:T(8,128)(2,1)}, u32[]{:S(2)}) copy-start(bf16[8,4096]{1,0:T(8,128)(2,1)} %param.7) | copy-start | bytes 196612
  228.8 414.3 %collective-permute-start = (bf16[8,1024]{0,1:T(8,128)(2,1)S(1)}, bf16[8,1024]{0,1:T(8,128)(2,1)}, u32[]{:S(2)}, u32[]{:S(2)}) collective-permute-start(bf16[8,1024]{0,1:T(8,128)(2,1)S(1)} %copy.67), channel_id=1, source_target_pairs={{0,128},{32,160},{64,192},{96,224},{1,129},{33,161},{65,193},{97,2... | collective-permute-start | bytes 49160 | tf_op jit(solution)/shard_map/ppermute | solution.py:10
  635.7 16.3 %copy-start.2 = (bf16[8,256,256]{2,1,0:T(8,128)(2,1)S(1)}, bf16[8,256,256]{2,1,0:T(8,128)(2,1)}, u32[]{:S(2)}) copy-start(bf16[8,256,256]{2,1,0:T(8,128)(2,1)} %rev.53) | copy-start | bytes 3145732
  635.7 16.7 %copy-start.3 = (bf16[8,256,256]{2,1,0:T(8,128)(2,1)S(1)}, bf16[8,256,256]{2,1,0:T(8,128)(2,1)}, u32[]{:S(2)}) copy-start(bf16[8,256,256]{2,1,0:T(8,128)(2,1)} %rev.54) | copy-start | bytes 3145732
  635.7 8.5 %collective-permute-start.1 = (bf16[8,1024]{0,1:T(8,128)(2,1)S(1)}, bf16[8,1024]{0,1:T(8,128)(2,1)}, u32[]{:S(2)}, u32[]{:S(2)}) collective-permute-start(bf16[8,1024]{0,1:T(8,128)(2,1)S(1)} %copy.67), channel_id=1, source_target_pairs={{0,96},{32,128},{64,160},{96,192},{128,224},{1,97},{33,129},{65,16... | collective-permute-start | bytes 49160 | tf_op jit(solution)/shard_map/ppermute | solution.py:10
  637.8 11.6 %collective-permute-start.2 = (bf16[8,1024]{0,1:T(8,128)(2,1)S(1)}, bf16[8,1024]{0,1:T(8,128)(2,1)}, u32[]{:S(2)}, u32[]{:S(2)}) collective-permute-start(bf16[8,1024]{0,1:T(8,128)(2,1)S(1)} %copy.67), channel_id=1, source_target_pairs={{0,64},{32,96},{64,128},{96,160},{128,192},{160,224},{1,65},{33,97... | collective-permute-start | bytes 49160 | tf_op jit(solution)/shard_map/ppermute | solution.py:10
  641.0 9.5 %collective-permute-start.3 = (bf16[8,1024]{0,1:T(8,128)(2,1)S(1)}, bf16[8,1024]{0,1:T(8,128)(2,1)}, u32[]{:S(2)}, u32[]{:S(2)}) collective-permute-start(bf16[8,1024]{0,1:T(8,128)(2,1)S(1)} %copy.67), channel_id=1, source_target_pairs={{0,32},{32,64},{64,96},{96,128},{128,160},{160,192},{192,224},{1,3... | collective-permute-start | bytes 49160 | tf_op jit(solution)/shard_map/ppermute | solution.py:10
  651.6 1.2 copy-start.4
  651.6 1.6 copy-start.5
  652.0 1.6 copy-start.6
  652.4 1.6 copy-start.7
  652.8 1.5 copy-start.8
  653.2 1.6 copy-start.9
  653.6 1.6 copy-start.10
  654.0 1.6 copy-start.11
  654.3 1.6 copy-start.12
  654.7 1.6 copy-start.13
  655.1 1.6 copy-start.14
  655.5 1.6 copy-start.15
  655.9 1.6 copy-start.16
  656.3 1.6 copy-start.17
  657.1 49.4 %copy-start.18 = (bf16[256,256]{1,0:T(8,128)(2,1)S(1)}, bf16[256,256]{1,0:T(8,128)(2,1)}, u32[]{:S(2)}) copy-start(bf16[256,256]{1,0:T(8,128)(2,1)} %param.6) | copy-start | bytes 393220
  657.1 50.6 %copy-start.1 = (bf16[1024,256]{1,0:T(8,128)(2,1)S(1)}, bf16[1024,256]{1,0:T(8,128)(2,1)}, u32[]{:S(2)}) copy-start(bf16[1024,256]{1,0:T(8,128)(2,1)} %param.4) | copy-start | bytes 1572868
  (18 other events, 21.9 us)
Sparse Core Ops, SparseCore 0:
  11.8 216.0 reduce-scatter.3
where the time goes:
time: 729 us; the launch traced here: 715 us
  local copies, waits for them, and re-layouts  409 us (56%)
  waiting for transfers between devices  220 us (30%)
  blocking collectives  48.2 us (7%)
  between operations  14.2 us (2%)
  starting transfers between devices  12.9 us (2%)
  matrix products  10.4 us (1%)
    unnamed x2, waiting for transfers between devices  216 us
    rev x17, local copies, waits for them, and re-layouts, banded_convolution_tile(): return jnp.flip(skewed[:, :, :width], axis=2)  184 us
    reshape x17, local copies, waits for them, and re-layouts, banded_convolution_tile(): tiled[:, :width * (2 * width + 1)].reshape(own, width, 2 * width + 1)  113 us
    unnamed x64, local copies, waits for them, and re-layouts  79.6 us
    all_gather x1, blocking collectives, per_device(): lax.all_gather(kernel_taps_per_mode, 'port', axis=0, tiled=True)  48.2 us
    slice x34, local copies, waits for them, and re-layouts, banded_convolution_tile(): return jnp.flip(skewed[:, :, :width], axis=2)  20.8 us
  transfers between devices with their start and end apart: 5, of which 2 were waited for; matrix products, arithmetic and copies ran while one was open for 54% of the time, Pallas kernels for 0%

commit v1 on v0

v1 whole, which is shorter than its diff:
```python
import functools

import jax
import jax.numpy as jnp
from jax import lax
from jax.experimental import pallas as pl
from jax.experimental.pallas import tpu as pltpu
from jax.sharding import PartitionSpec as P

LANES = 128
SUB = 8
STEP = 32
PER_TILE = LANES // STEP


def flipping_matrix():
    row = lax.broadcasted_iota(jnp.int32, (LANES, LANES), 0)
    col = lax.broadcasted_iota(jnp.int32, (LANES, LANES), 1)
    return jnp.where(row + col == LANES - 1, 1.0, 0.0).astype(jnp.bfloat16)


def toeplitz_kernel(tiles, depth, taps_ref, out_ref):
    modes = taps_ref.shape[0]
    stacked = jnp.concatenate(
        [taps_ref[:, LANES * (tiles - 1 - j) : LANES * (tiles - j)].astype(jnp.float32) for j in range(tiles)], axis=0
    )
    flipped = jnp.dot(stacked.astype(jnp.bfloat16), flipping_matrix(), preferred_element_type=jnp.float32)
    lane = lax.broadcasted_iota(jnp.int32, (SUB, LANES), 1)
    sub = lax.broadcasted_iota(jnp.int32, (SUB, LANES), 0)
    groups = STEP // SUB
    zero = jnp.zeros((SUB, LANES), jnp.float32)
    for m in range(modes):
        before = [zero] * groups
        for j in range(depth // LANES):
            if j < tiles:
                line = jnp.broadcast_to(flipped[modes * j + m : modes * j + m + 1, :], (SUB, LANES))
                now = [pltpu.roll(line, SUB * g + 1, 1, stride=1, stride_axis=0) for g in range(groups)]
            else:
                now = [zero] * groups
            parts = [
                jnp.where(lane < sub + (SUB * g + 1), before[g], now[g]) if j <= tiles else zero for g in range(groups)
            ]
            out_ref[STEP * m : STEP * (m + 1), LANES * j : LANES * (j + 1)] = jnp.concatenate(parts, axis=0).astype(
                out_ref.dtype
            )
            before = now


def projection_kernel(parts_ref, own_ref, other_ref, out_ref):
    merged = jnp.sum(parts_ref[...], axis=0)
    high = merged.astype(jnp.bfloat16).astype(jnp.float32)
    rest = merged - high
    middle = rest.astype(jnp.bfloat16).astype(jnp.float32)
    low = rest - middle
    modes = merged.shape[0]
    weights = jnp.concatenate([high, middle, low, jnp.zeros_like(low)], axis=0).astype(jnp.bfloat16)
    contract = (((1,), (1,)), ((), ()))

    def modal(ref):
        terms = lax.dot_general(weights, ref[...], contract, preferred_element_type=jnp.float32)
        return terms[:modes] + (terms[modes : 2 * modes] + terms[2 * modes : 3 * modes])

    own, other = modal(own_ref), modal(other_ref)
    first = lax.rem(lax.axis_index("tm"), 2) == 0
    span = own.shape[1]
    out_ref[:, :span] = jnp.where(first, own, other).astype(out_ref.dtype)
    out_ref[:, span:] = jnp.where(first, other, own).astype(out_ref.dtype)


def convolution_kernel(tap_tiles, copies, back2_ref, back1_ref, pair_ref, toeplitz_ref, out_ref, hankel):
    place = lax.axis_index("tm")
    chip, second = place // 2, lax.rem(place, 2) == 1
    modes, pair = pair_ref.shape
    span = pair // 2
    out_tiles = span // LANES
    older = jnp.where(chip >= 2, back2_ref[...].astype(jnp.float32), 0.0)
    newer = jnp.where(chip >= 1, back1_ref[...].astype(jnp.float32), 0.0)
    every = jnp.concatenate([older, newer, pair_ref[...].astype(jnp.float32)], axis=1)
    window = span + tap_tiles * LANES
    window = jnp.where(second, every[:, span : span + window], every[:, :window])
    count = window.shape[1] // LANES
    tiles = [window[:, LANES * t : LANES * (t + 1)] for t in range(count)]
    lane = lax.broadcasted_iota(jnp.int32, (SUB, LANES), 1)
    zero = jnp.zeros((SUB, LANES), jnp.float32)
    rolled = [[tile] + [pltpu.roll(tile, LANES - STEP * j, 1) for j in range(1, PER_TILE)] for tile in tiles]
    rolled.append([zero] * PER_TILE)
    for t in range(count):
        rows = [tiles[t]] + [
            jnp.where(lane < LANES - STEP * j, rolled[t][j], rolled[t + 1][j]) for j in range(1, PER_TILE)
        ]
        hankel[t] = jnp.concatenate(rows, axis=0).astype(hankel.dtype)
    for t in range(count, hankel.shape[0]):
        hankel[t] = jnp.zeros(hankel.shape[1:], hankel.dtype)
    depth = toeplitz_ref.shape[1]
    rows = out_tiles * PER_TILE * modes
    contract = (((1,), (1,)), ((), ()))
    total = jnp.zeros((rows, STEP * modes), jnp.float32)
    for c in range(0, depth // LANES, 2):
        left = jnp.concatenate(
            [hankel[c + k : c + k + out_tiles].reshape(rows, LANES) for k in range(2)], axis=1
        )
        total = total + lax.dot_general(
            left, toeplitz_ref[:, LANES * c : LANES * (c + 2)], contract, preferred_element_type=jnp.float32
        )
    sub = lax.broadcasted_iota(jnp.int32, (SUB, LANES), 0)
    place_in_tile, column = sub % PER_TILE, lane // STEP
    for g in range(out_tiles):
        picked = []
        for j in range(PER_TILE):
            row = (g * PER_TILE + j) * modes
            block = total[row : row + modes]
            own = block[:, :LANES]
            for h in range(1, STEP * modes // LANES):
                own = jnp.where(sub // PER_TILE == h, block[:, LANES * h : LANES * (h + 1)], own)
            picked.append(own)
        tile = zero
        for d in range(PER_TILE):
            line = picked[d]
            for s in range(1, PER_TILE):
                line = jnp.where(place_in_tile == s, picked[(s + d) % PER_TILE], line)
            if d:
                line = pltpu.roll(line, STEP * d, 1)
            tile = jnp.where(column == (place_in_tile + d) % PER_TILE, line, tile)
        tile = tile.astype(out_ref.dtype)
        for k in range(copies):
            out_ref[k, :, LANES * g : LANES * (g + 1)] = tile


def on_chip(kernel, shape, dtype, scratch=(), flops=0, bytes_accessed=0):
    return pl.pallas_call(
        kernel,
        out_shape=jax.ShapeDtypeStruct(shape, dtype),
        scratch_shapes=scratch,
        compiler_params=pltpu.CompilerParams(vmem_limit_bytes=40 * 1024 * 1024),
        cost_estimate=pl.CostEstimate(flops=flops, bytes_accessed=bytes_accessed, transcendentals=0),
    )


def per_device(ports, steps, counters, signatures, eigen_vectors_at_pins, taps):
    modes, span = taps.shape
    cycles, tallies = counters.shape
    swap = [(i, i ^ 1) for i in range(steps)]
    other = lax.ppermute(counters, "tm", swap)
    partial = jnp.einsum("cp,pm->mc", signatures, eigen_vectors_at_pins, preferred_element_type=jnp.float32)
    parts = lax.all_to_all(partial.reshape(ports, modes, tallies), "port", 0, 0, tiled=True)
    tap_tiles = span // LANES
    depth = (tap_tiles + 2) * LANES
    toeplitz = on_chip(
        functools.partial(toeplitz_kernel, tap_tiles, depth),
        (STEP * modes, depth),
        jnp.bfloat16,
        flops=2 * 10**9,
        bytes_accessed=2 * STEP * modes * depth,
    )(taps)
    pair = on_chip(projection_kernel, (modes, 2 * cycles), jnp.bfloat16)(parts, counters, other)
    back1 = lax.ppermute(pair, "tm", [(i, (i + 2) % steps) for i in range(steps)])
    back2 = lax.ppermute(pair, "tm", [(i, (i + 4) % steps) for i in range(steps)])
    responses = on_chip(
        functools.partial(convolution_kernel, tap_tiles, ports),
        (ports, modes, cycles),
        jnp.bfloat16,
        scratch=[pltpu.VMEM((tap_tiles + 1 + cycles // LANES + 1, PER_TILE * modes, LANES), jnp.bfloat16)],
    )(back2, back1, pair, toeplitz)
    complete = lax.all_to_all(responses, "port", 0, 0, tiled=True).reshape(ports * modes, cycles)
    return jnp.einsum("vm,uv->mu", complete, eigen_vectors_at_pins, preferred_element_type=jnp.float32).astype(
        jnp.bfloat16
    )


def solution(mesh):
    in_specs = (P("tm", None), P(None, "port"), P("port", None), P("port", None))
    body = functools.partial(per_device, mesh.shape["port"], mesh.shape["tm"])
    return jax.shard_map(body, mesh=mesh, in_specs=in_specs, out_specs=P("tm", "port"), check_vma=False)
```

time: 729 us -> 56 us (0.08); the launches traced: 715 us -> 55.7 us
  local copies, waits for them, and re-layouts: 409 us -> 1.94 us
  waiting for transfers between devices: 220 us -> 1.93 us
  between operations: 14.2 us -> 0.04 us
  starting transfers between devices: 12.9 us -> 4.29 us
  matrix products: 10.4 us -> 2.27 us
    unnamed x2 -> x0, waiting for transfers between devices: 216 us -> none
    rev x17 -> x0, local copies, waits for them, and re-layouts: 184 us -> none  [banded_convolution_tile(): return jnp.flip(skewed[:, :, :width], axis=2)]
    reshape x17 -> x0, local copies, waits for them, and re-layouts: 113 us -> none  [banded_convolution_tile(): tiled[:, :width * (2 * width + 1)].reshape(own, width, 2 * width + 1)]
    unnamed x64 -> x6, local copies, waits for them, and re-layouts: 79.6 us -> 1.94 us
    all_gather x1 -> x0, blocking collectives: 48.2 us -> none  [per_device(): lax.all_gather(kernel_taps_per_mode, 'port', axis=0, tiled=True)]
    all_to_all x0 -> x2, blocking collectives: none -> 43.1 us  [the longest x1 23.4 us: per_device(): lax.all_to_all(partial.reshape(ports, modes, tallies), 'port', 0, 0, tile...]
    slice x53 -> x0, local copies, waits for them, and re-layouts: 26.2 us -> none  [the longest x34 20.8 us: banded_convolution_tile(): return jnp.flip(skewed[:, :, :width], axis=2)]
    ppermute x4 -> x3, starting transfers between devices: 12.9 us -> 4.29 us  [the longest x1 2.73 us: per_device(): lax.ppermute(pair, 'tm', [(i, (i + 4) % steps) for i in range(steps)])]
  transfers between devices with their start and end apart: 5 -> 3, of which waited for: 2 -> 2; matrix products, arithmetic and copies ran while one was open for 54% -> 2% of each run, Pallas kernels for 0% -> 1%
where the time goes in v1:
time: 56 us; the launch traced here: 55.7 us
  blocking collectives  43.1 us (77%)
  starting transfers between devices  4.29 us (8%)
  matrix products  2.27 us (4%)
  Pallas kernels  2.13 us (4%)
  local copies, waits for them, and re-layouts  1.94 us (3%)
  waiting for transfers between devices  1.93 us (3%)
    all_to_all x1, blocking collectives, per_device(): lax.all_to_all(partial.reshape(ports, modes, tallies), 'port', 0, 0, tile...  23.4 us
    all_to_all x1, blocking collectives, per_device(): lax.all_to_all(responses, 'port', 0, 0, tiled=True)  19.7 us
    ppermute x1, starting transfers between devices, per_device(): lax.ppermute(pair, 'tm', [(i, (i + 4) % steps) for i in range(steps)])  2.73 us
    unnamed x6, local copies, waits for them, and re-layouts  1.94 us
    ppermute x1, waiting for transfers between devices, per_device(): lax.ppermute(pair, 'tm', [(i, (i + 4) % steps) for i in range(steps)])  1.78 us
    ppermute x1, starting transfers between devices, per_device(): lax.ppermute(pair, 'tm', [(i, (i + 2) % steps) for i in range(steps)])  1.56 us
    dot_general x1, matrix products, per_device(): jnp.einsum('vm,uv->mu', complete, eigen_vectors_at_pins, preferred_elemen...  1.15 us
  transfers between devices with their start and end apart: 3, of which 2 were waited for; matrix products, arithmetic and copies ran while one was open for 2% of the time, Pallas kernels for 1%

profile of v1, /device:TPU:32, one launch (start us, length us, event | category | flops | bytes accessed | tf_op | source)
XLA Modules:
  0.0 55.7 jit_solution(10976266955351041302)
XLA Ops:
  0.0 0.0 copy-start
  0.0 0.0 copy-start.2
  0.0 0.0 collective-permute-start
  0.0 0.9 %copy-done = bf16[256,256]{1,0:T(8,128)(2,1)S(1)} copy-done((bf16[256,256]{1,0:T(8,128)(2,1)S(1)}, bf16[256,256]{1,0:T(8,128)(2,1)}, u32[]{:S(2)}) %copy-start) | copy-done | bytes 131096
  0.9 1.1 %convolution_bitcast_fusion = f32[32,8,256]{2,1,0:T(8,128)S(1)} fusion(bf16[256,256]{1,0:T(8,128)(2,1)S(1)} %copy-done, bf16[256,256]{1,0:T(8,128)(2,1)} %param.5), kind=kOutput, calls=%fused_computation.1 | convolution fusion | flops 33554432 | bytes 524288 | tf_op jit(solution)/shard_map/cp,pm->mc/dot_general | solution.py:144
  2.0 23.4 %all_to_all.10.parts_ref = f32[32,8,256]{2,1,0:T(8,128)S(1)} all-to-all(f32[32,8,256]{2,1,0:T(8,128)S(1)} %convolution_bitcast_fusion), channel_id=1, replica_groups=mesh['tm'=8,'port'=32] {'port'}, dimensions={0} | all-to-all | bytes 524288 | tf_op jit(solution)/shard_map/all_to_all | solution.py:145
  25.5 0.0 collective-permute-done.other_ref
  25.5 0.0 copy-start.1
  25.5 1.0 %copy-done.1 = bf16[1024,256]{1,0:T(8,128)(2,1)S(1)} copy-done((bf16[1024,256]{1,0:T(8,128)(2,1)S(1)}, bf16[1024,256]{1,0:T(8,128)(2,1)}, u32[]{:S(2)}) %copy-start.1) | copy-done | bytes 524312
  26.5 0.4 shard_map.46.pair_ref
  26.9 1.6 %collective-permute-start.2 = (bf16[8,2048]{1,0:T(8,128)(2,1)S(1)}, bf16[8,2048]{1,0:T(8,128)(2,1)S(1)}, u32[]{:S(2)}, u32[]{:S(2)}) collective-permute-start(bf16[8,2048]{1,0:T(8,128)(2,1)S(1)} %shard_map.46.pair_ref), channel_id=1, source_target_pairs={{0,64},{32,96},{64,128},{96,160},{128,192},{160,224},{192,0},{224,... | collective-permute-start | bytes 98312 | tf_op jit(solution)/shard_map/ppermute | solution.py:156
  28.5 2.7 %collective-permute-start.1 = (bf16[8,2048]{1,0:T(8,128)(2,1)S(1)}, bf16[8,2048]{1,0:T(8,128)(2,1)S(1)}, u32[]{:S(2)}, u32[]{:S(2)}) collective-permute-start(bf16[8,2048]{1,0:T(8,128)(2,1)S(1)} %shard_map.46.pair_ref), channel_id=1, source_target_pairs={{0,128},{32,160},{64,192},{96,224},{128,0},{160,32},{192,64},{224,... | collective-permute-start | bytes 98312 | tf_op jit(solution)/shard_map/ppermute | solution.py:157
  31.2 0.0 copy-done.2
  31.2 0.8 %shard_map.47.toeplitz_ref = bf16[256,4352]{1,0:T(8,128)(2,1)S(1)} custom-call(bf16[8,4096]{1,0:T(8,128)(2,1)S(1)} %copy-done.2), custom_call_target="tpu_custom_call" | custom-call | flops 2000000000 | bytes 2228224 | tf_op jit(solution)/shard_map/pallas_call | solution.py:148
  32.0 0.1 collective-permute-done.2.back1_ref
  32.1 1.8 %collective-permute-done.1.back2_ref = bf16[8,2048]{1,0:T(8,128)(2,1)S(1)} collective-permute-done((bf16[8,2048]{1,0:T(8,128)(2,1)S(1)}, bf16[8,2048]{1,0:T(8,128)(2,1)S(1)}, u32[]{:S(2)}, u32[]{:S(2)}) %collective-permute-start.1) | collective-permute-done | bytes 32800 | tf_op jit(solution)/shard_map/ppermute | solution.py:157
  33.9 1.0 %shard_map.48 = bf16[32,8,1024]{2,1,0:T(8,128)(2,1)S(1)} custom-call(bf16[8,2048]{1,0:T(8,128)(2,1)S(1)} %collective-permute-done.1.back2_ref, bf16[8,2048]{1,0:T(8,128)(2,1)S(1)} %collective-permute-done.2.back1_ref, bf16[8,2048]{1,0:T(8,128)(2,1)S(1)} %shard_map.46.pair_ref, bf16[256,4352]{1,0:T(8,128)(2,1)S(1)} %shard_map.47.toeplitz_ref), custom_call_target="tpu_custom_call" | custom-call | tf_op jit(solution)/shard_map/pallas_call | solution.py:158
  34.9 19.7 %all_to_all.11 = bf16[32,8,1024]{2,1,0:T(8,128)(2,1)S(1)} all-to-all(bf16[32,8,1024]{2,1,0:T(8,128)(2,1)S(1)} %shard_map.48), channel_id=1, replica_groups=mesh['tm'=8,'port'=32] {'port'}, dimensions={0} | all-to-all | bytes 1048576 | tf_op jit(solution)/shard_map/all_to_all | solution.py:164
  54.6 1.1 %convolution_convert_fusion = bf16[1024,256]{1,0:T(8,128)(2,1)} fusion(bf16[256,256]{1,0:T(8,128)(2,1)S(1)} %copy-done, bf16[32,8,1024]{2,1,0:T(8,128)(2,1)S(1)} %all_to_all.11), kind=kOutput, calls=%fused_computation | convolution fusion | flops 134479872 | bytes 1179648 | tf_op jit(solution)/shard_map/vm,uv->mu/dot_general | solution.py:165
Async XLA Ops:
  0.0 0.9 %copy-start = (bf16[256,256]{1,0:T(8,128)(2,1)S(1)}, bf16[256,256]{1,0:T(8,128)(2,1)}, u32[]{:S(2)}) copy-start(bf16[256,256]{1,0:T(8,128)(2,1)} %param.6) | copy-start | bytes 393220
  0.0 31.2 %copy-start.2 = (bf16[8,4096]{1,0:T(8,128)(2,1)S(1)}, bf16[8,4096]{1,0:T(8,128)(2,1)}, u32[]{:S(2)}) copy-start(bf16[8,4096]{1,0:T(8,128)(2,1)} %taps_ref.1) | copy-start | bytes 196612
  0.0 25.5 %collective-permute-start = (bf16[1024,256]{1,0:T(8,128)(2,1)}, bf16[1024,256]{1,0:T(8,128)(2,1)S(1)}, u32[]{:S(2)}, u32[]{:S(2)}) collective-permute-start(bf16[1024,256]{1,0:T(8,128)(2,1)} %own_ref.1), channel_id=1, source_target_pairs={{0,32},{32,0},{64,96},{96,64},{128,160},{160,128},{192,224},{224,1... | collective-permute-start | bytes 1572872 | tf_op jit(solution)/shard_map/ppermute | solution.py:143
  25.5 1.0 %copy-start.1 = (bf16[1024,256]{1,0:T(8,128)(2,1)S(1)}, bf16[1024,256]{1,0:T(8,128)(2,1)}, u32[]{:S(2)}) copy-start(bf16[1024,256]{1,0:T(8,128)(2,1)} %own_ref.1) | copy-start | bytes 1572868
  26.9 5.2 %collective-permute-start.2 = (bf16[8,2048]{1,0:T(8,128)(2,1)S(1)}, bf16[8,2048]{1,0:T(8,128)(2,1)S(1)}, u32[]{:S(2)}, u32[]{:S(2)}) collective-permute-start(bf16[8,2048]{1,0:T(8,128)(2,1)S(1)} %shard_map.46.pair_ref), channel_id=1, source_target_pairs={{0,64},{32,96},{64,128},{96,160},{128,192},{160,224},{192,0},{224,... | collective-permute-start | bytes 98312 | tf_op jit(solution)/shard_map/ppermute | solution.py:156
  28.5 5.4 %collective-permute-start.1 = (bf16[8,2048]{1,0:T(8,128)(2,1)S(1)}, bf16[8,2048]{1,0:T(8,128)(2,1)S(1)}, u32[]{:S(2)}, u32[]{:S(2)}) collective-permute-start(bf16[8,2048]{1,0:T(8,128)(2,1)S(1)} %shard_map.46.pair_ref), channel_id=1, source_target_pairs={{0,128},{32,160},{64,192},{96,224},{128,0},{160,32},{192,64},{224,... | collective-permute-start | bytes 98312 | tf_op jit(solution)/shard_map/ppermute | solution.py:157

commit v2 on v1

--- a/solution.py
+++ b/solution.py
@@ -46,8 +46,25 @@
             before = now
 
 
+def merging_kernel(signatures_hbm, modes_hbm, counters_hbm, partial_ref, counters_ref, signatures_ref, modes_ref, sems):
+    copies = [
+        pltpu.make_async_copy(signatures_hbm, signatures_ref, sems.at[0]),
+        pltpu.make_async_copy(modes_hbm, modes_ref, sems.at[1]),
+        pltpu.make_async_copy(counters_hbm, counters_ref, sems.at[2]),
+    ]
+    for copy in copies:
+        copy.start()
+    copies[0].wait()
+    copies[1].wait()
+    partial = lax.dot_general(
+        modes_ref[...], signatures_ref[...], (((0,), (1,)), ((), ())), preferred_element_type=jnp.float32
+    )
+    partial_ref[...] = partial.reshape(partial_ref.shape).astype(partial_ref.dtype)
+    copies[2].wait()
+
+
 def projection_kernel(parts_ref, own_ref, other_ref, out_ref):
-    merged = jnp.sum(parts_ref[...], axis=0)
+    merged = jnp.sum(parts_ref[...].astype(jnp.float32), axis=0)
     high = merged.astype(jnp.bfloat16).astype(jnp.float32)
     rest = merged - high
     middle = rest.astype(jnp.bfloat16).astype(jnp.float32)
@@ -141,8 +158,24 @@
     cycles, tallies = counters.shape
     swap = [(i, i ^ 1) for i in range(steps)]
     other = lax.ppermute(counters, "tm", swap)
-    partial = jnp.einsum("cp,pm->mc", signatures, eigen_vectors_at_pins, preferred_element_type=jnp.float32)
-    parts = lax.all_to_all(partial.reshape(ports, modes, tallies), "port", 0, 0, tiled=True)
+    in_hbm = pl.BlockSpec(memory_space=pltpu.HBM)
+    in_vmem = pl.BlockSpec(memory_space=pltpu.VMEM)
+    partial, held = pl.pallas_call(
+        merging_kernel,
+        out_shape=(
+            jax.ShapeDtypeStruct((ports, modes, tallies), jnp.bfloat16),
+            jax.ShapeDtypeStruct(counters.shape, counters.dtype),
+        ),
+        in_specs=[in_hbm] * 3,
+        out_specs=(in_vmem, in_vmem),
+        scratch_shapes=[
+            pltpu.VMEM(signatures.shape, signatures.dtype),
+            pltpu.VMEM(eigen_vectors_at_pins.shape, eigen_vectors_at_pins.dtype),
+            pltpu.SemaphoreType.DMA((3,)),
+        ],
+        compiler_params=pltpu.CompilerParams(vmem_limit_bytes=16 * 1024 * 1024),
+    )(*[pltpu.with_memory_space_constraint(x, pltpu.HBM) for x in (signatures, eigen_vectors_at_pins, counters)])
+    parts = lax.all_to_all(partial, "port", 0, 0, tiled=True)
     tap_tiles = span // LANES
     depth = (tap_tiles + 2) * LANES
     toeplitz = on_chip(
@@ -152,9 +185,9 @@
         flops=2 * 10**9,
         bytes_accessed=2 * STEP * modes * depth,
     )(taps)
-    pair = on_chip(projection_kernel, (modes, 2 * cycles), jnp.bfloat16)(parts, counters, other)
+    pair = on_chip(projection_kernel, (modes, 2 * cycles), jnp.bfloat16)(parts, held, other)
+    back2 = lax.ppermute(pair, "tm", [(i, (i + 4) % steps) for i in range(steps)])
     back1 = lax.ppermute(pair, "tm", [(i, (i + 2) % steps) for i in range(steps)])
-    back2 = lax.ppermute(pair, "tm", [(i, (i + 4) % steps) for i in range(steps)])
     responses = on_chip(
         functools.partial(convolution_kernel, tap_tiles, ports),
         (ports, modes, cycles),

time: 56 us -> 52.5 us (0.938)
  local copies, waits for them, and re-layouts: 1.94 us -> 0.01 us
  blocking collectives: 43.1 us -> 41.6 us
  Pallas kernels: 2.13 us -> 3.39 us
  matrix products: 2.27 us -> 1.15 us
    unnamed x6 -> x4, local copies, waits for them, and re-layouts: 1.94 us -> 0.01 us
    all_to_all x1, blocking collectives: 23.4 us -> 21.5 us  [per_device(): parts = lax.all_to_all(partial, 'port', 0, 0, tiled=True)]
    pallas_call x0 -> x1, Pallas kernels: none -> 1.25 us  [per_device(): pl.pallas_call(merging_kernel, out_shape=(jax.ShapeDtypeStruct((ports, mo...]
    dot_general x1 -> x0, matrix products: 1.12 us -> none  [per_device(): jnp.einsum('cp,pm->mc', signatures, eigen_vectors_at_pins, preferred_elem...]
  transfers between devices with their start and end apart: 3 -> 3, of which waited for: 2 -> 2; matrix products, arithmetic and copies ran while one was open for 2% -> 0% of each run, Pallas kernels for 1% -> 4%
where the time goes in v2:
time: 52.5 us; the launch traced here: 52.4 us
  blocking collectives  41.6 us (79%)
  starting transfers between devices  4.29 us (8%)
  Pallas kernels  3.39 us (6%)
  waiting for transfers between devices  1.91 us (4%)
  matrix products  1.15 us (2%)
    all_to_all x1, blocking collectives, per_device(): parts = lax.all_to_all(partial, 'port', 0, 0, tiled=True)  21.5 us
    all_to_all x1, blocking collectives, per_device(): lax.all_to_all(responses, 'port', 0, 0, tiled=True)  20 us
    ppermute x1, starting transfers between devices, per_device(): lax.ppermute(pair, 'tm', [(i, (i + 4) % steps) for i in range(steps)])  2.73 us
    ppermute x1, waiting for transfers between devices, per_device(): lax.ppermute(pair, 'tm', [(i, (i + 4) % steps) for i in range(steps)])  1.56 us
    ppermute x1, starting transfers between devices, per_device(): lax.ppermute(pair, 'tm', [(i, (i + 2) % steps) for i in range(steps)])  1.56 us
    pallas_call x1, Pallas kernels, per_device(): pl.pallas_call(merging_kernel, out_shape=(jax.ShapeDtypeStruct((ports, mo...  1.25 us
    dot_general x1, matrix products, per_device(): jnp.einsum('vm,uv->mu', complete, eigen_vectors_at_pins, preferred_elemen...  1.15 us
  transfers between devices with their start and end apart: 3, of which 2 were waited for; matrix products, arithmetic and copies ran while one was open for 0% of the time, Pallas kernels for 4%

profile of v2, /device:TPU:32, one launch (start us, length us, event | category | flops | bytes accessed | tf_op | source)
XLA Modules:
  0.0 52.4 jit_solution(933596607758168018)
XLA Ops:
  0.0 0.0 copy-start
  0.0 0.0 collective-permute-start
  0.0 1.3 %shard_map.46 = (bf16[32,8,256]{2,1,0:T(8,128)(2,1)S(1)}, bf16[1024,256]{1,0:T(8,128)(2,1)S(1)}) custom-call(bf16[256,256]{1,0:T(8,128)(2,1)} %signatures_hbm.1, bf16[256,256]{1,0:T(8,128)(2,1)} %modes_hbm.1, bf16[1024,256]{1,0:T(8,128)(2,1)} %counters_hbm.1), custom_call_target="tpu_custom_call" | custom-call | tf_op jit(solution)/shard_map/pallas_call | solution.py:163
  1.3 21.5 %all_to_all.10.parts_ref = bf16[32,8,256]{2,1,0:T(8,128)(2,1)S(1)} all-to-all(bf16[32,8,256]{2,1,0:T(8,128)(2,1)S(1)} %get-tuple-element.7), channel_id=1, replica_groups=mesh['tm'=8,'port'=32] {'port'}, dimensions={0} | all-to-all | bytes 262144 | tf_op jit(solution)/shard_map/all_to_all | solution.py:178
  22.8 0.0 collective-permute-done.other_ref
  22.8 0.4 shard_map.47.pair_ref
  23.2 1.6 %collective-permute-start.2 = (bf16[8,2048]{1,0:T(8,128)(2,1)S(1)}, bf16[8,2048]{1,0:T(8,128)(2,1)S(1)}, u32[]{:S(2)}, u32[]{:S(2)}) collective-permute-start(bf16[8,2048]{1,0:T(8,128)(2,1)S(1)} %shard_map.47.pair_ref), channel_id=1, source_target_pairs={{0,64},{32,96},{64,128},{96,160},{128,192},{160,224},{192,0},{224,... | collective-permute-start | bytes 98312 | tf_op jit(solution)/shard_map/ppermute | solution.py:190
  24.8 2.7 %collective-permute-start.1 = (bf16[8,2048]{1,0:T(8,128)(2,1)S(1)}, bf16[8,2048]{1,0:T(8,128)(2,1)S(1)}, u32[]{:S(2)}, u32[]{:S(2)}) collective-permute-start(bf16[8,2048]{1,0:T(8,128)(2,1)S(1)} %shard_map.47.pair_ref), channel_id=1, source_target_pairs={{0,128},{32,160},{64,192},{96,224},{128,0},{160,32},{192,64},{224,... | collective-permute-start | bytes 98312 | tf_op jit(solution)/shard_map/ppermute | solution.py:189
  27.5 0.0 copy-done
  27.5 0.8 %shard_map.48.toeplitz_ref = bf16[256,4352]{1,0:T(8,128)(2,1)S(1)} custom-call(bf16[8,4096]{1,0:T(8,128)(2,1)S(1)} %copy-done), custom_call_target="tpu_custom_call" | custom-call | flops 2000000000 | bytes 2228224 | tf_op jit(solution)/shard_map/pallas_call | solution.py:181
  28.3 0.0 copy-start.1
  28.3 0.3 collective-permute-done.2.back1_ref
  28.6 1.6 %collective-permute-done.1.back2_ref = bf16[8,2048]{1,0:T(8,128)(2,1)S(1)} collective-permute-done((bf16[8,2048]{1,0:T(8,128)(2,1)S(1)}, bf16[8,2048]{1,0:T(8,128)(2,1)S(1)}, u32[]{:S(2)}, u32[]{:S(2)}) %collective-permute-start.1) | collective-permute-done | bytes 32800 | tf_op jit(solution)/shard_map/ppermute | solution.py:189
  30.2 1.0 %shard_map.49 = bf16[32,8,1024]{2,1,0:T(8,128)(2,1)S(1)} custom-call(bf16[8,2048]{1,0:T(8,128)(2,1)S(1)} %collective-permute-done.1.back2_ref, bf16[8,2048]{1,0:T(8,128)(2,1)S(1)} %collective-permute-done.2.back1_ref, bf16[8,2048]{1,0:T(8,128)(2,1)S(1)} %shard_map.47.pair_ref, bf16[256,4352]{1,0:T(8,128)(2,1)S(1)} %shard_map.48.toeplitz_ref), custom_call_target="tpu_custom_call" | custom-call | tf_op jit(solution)/shard_map/pallas_call | solution.py:191
  31.2 20.0 %all_to_all.11 = bf16[32,8,1024]{2,1,0:T(8,128)(2,1)S(1)} all-to-all(bf16[32,8,1024]{2,1,0:T(8,128)(2,1)S(1)} %shard_map.49), channel_id=1, replica_groups=mesh['tm'=8,'port'=32] {'port'}, dimensions={0} | all-to-all | bytes 1048576 | tf_op jit(solution)/shard_map/all_to_all | solution.py:197
  51.2 0.0 copy-done.1
  51.2 1.1 %convolution_convert_fusion = bf16[1024,256]{1,0:T(8,128)(2,1)} fusion(bf16[256,256]{1,0:T(8,128)(2,1)S(1)} %copy-done.1, bf16[32,8,1024]{2,1,0:T(8,128)(2,1)S(1)} %all_to_all.11), kind=kOutput, calls=%fused_computation | convolution fusion | flops 134479872 | bytes 1179648 | tf_op jit(solution)/shard_map/vm,uv->mu/dot_general | solution.py:198
Async XLA Ops:
  0.0 27.5 %copy-start = (bf16[8,4096]{1,0:T(8,128)(2,1)S(1)}, bf16[8,4096]{1,0:T(8,128)(2,1)}, u32[]{:S(2)}) copy-start(bf16[8,4096]{1,0:T(8,128)(2,1)} %taps_ref.1) | copy-start | bytes 196612
  0.0 22.8 %collective-permute-start = (bf16[1024,256]{1,0:T(8,128)(2,1)}, bf16[1024,256]{1,0:T(8,128)(2,1)S(1)}, u32[]{:S(2)}, u32[]{:S(2)}) collective-permute-start(bf16[1024,256]{1,0:T(8,128)(2,1)} %counters_hbm.1), channel_id=1, source_target_pairs={{0,32},{32,0},{64,96},{96,64},{128,160},{160,128},{192,224},{224,1... | collective-permute-start | bytes 1572872 | tf_op jit(solution)/shard_map/ppermute | solution.py:160
  23.2 5.4 %collective-permute-start.2 = (bf16[8,2048]{1,0:T(8,128)(2,1)S(1)}, bf16[8,2048]{1,0:T(8,128)(2,1)S(1)}, u32[]{:S(2)}, u32[]{:S(2)}) collective-permute-start(bf16[8,2048]{1,0:T(8,128)(2,1)S(1)} %shard_map.47.pair_ref), channel_id=1, source_target_pairs={{0,64},{32,96},{64,128},{96,160},{128,192},{160,224},{192,0},{224,... | collective-permute-start | bytes 98312 | tf_op jit(solution)/shard_map/ppermute | solution.py:190
  24.8 5.4 %collective-permute-start.1 = (bf16[8,2048]{1,0:T(8,128)(2,1)S(1)}, bf16[8,2048]{1,0:T(8,128)(2,1)S(1)}, u32[]{:S(2)}, u32[]{:S(2)}) collective-permute-start(bf16[8,2048]{1,0:T(8,128)(2,1)S(1)} %shard_map.47.pair_ref), channel_id=1, source_target_pairs={{0,128},{32,160},{64,192},{96,224},{128,0},{160,32},{192,64},{224,... | collective-permute-start | bytes 98312 | tf_op jit(solution)/shard_map/ppermute | solution.py:189
  28.3 22.9 %copy-start.1 = (bf16[256,256]{1,0:T(8,128)(2,1)S(1)}, bf16[256,256]{1,0:T(8,128)(2,1)}, u32[]{:S(2)}) copy-start(bf16[256,256]{1,0:T(8,128)(2,1)} %modes_hbm.1) | copy-start | bytes 393220

commit v3 on v2

--- a/solution.py
+++ b/solution.py
@@ -19,7 +19,7 @@
     return jnp.where(row + col == LANES - 1, 1.0, 0.0).astype(jnp.bfloat16)
 
 
-def toeplitz_kernel(tiles, depth, taps_ref, out_ref):
+def fill_toeplitz(tiles, depth, taps_ref, out_ref):
     modes = taps_ref.shape[0]
     stacked = jnp.concatenate(
         [taps_ref[:, LANES * (tiles - 1 - j) : LANES * (tiles - j)].astype(jnp.float32) for j in range(tiles)], axis=0
@@ -84,41 +84,68 @@
     out_ref[:, span:] = jnp.where(first, other, own).astype(out_ref.dtype)
 
 
-def convolution_kernel(tap_tiles, copies, back2_ref, back1_ref, pair_ref, toeplitz_ref, out_ref, hankel):
+def hankel_rows(tiles, following):
+    lane = lax.broadcasted_iota(jnp.int32, (SUB, LANES), 1)
+    moved = [[pltpu.roll(tile, LANES - STEP * j, 1) for j in range(1, PER_TILE)] for tile in [*tiles, following]]
+    for t, tile in enumerate(tiles):
+        rows = [tile] + [
+            jnp.where(lane < LANES - STEP * j, moved[t][j - 1], moved[t + 1][j - 1]) for j in range(1, PER_TILE)
+        ]
+        yield jnp.concatenate(rows, axis=0)
+
+
+def banded_product(total, hankel, first, toeplitz_ref, steps, out_tiles):
+    rows = total.shape[0]
+    for c in steps:
+        left = jnp.concatenate(
+            [hankel[c + k - first : c + k - first + out_tiles].reshape(rows, LANES) for k in range(2)], axis=1
+        )
+        total = total + lax.dot_general(
+            left,
+            toeplitz_ref[:, LANES * c : LANES * (c + 2)],
+            (((1,), (1,)), ((), ())),
+            preferred_element_type=jnp.float32,
+        )
+    return total
+
+
+def near_kernel(out_tiles, back1_ref, pair_ref, taps_ref, total_ref, hankel_ref, toeplitz_ref):
+    fill_toeplitz(taps_ref.shape[1] // LANES, toeplitz_ref.shape[1], taps_ref, toeplitz_ref)
     place = lax.axis_index("tm")
     chip, second = place // 2, lax.rem(place, 2) == 1
-    modes, pair = pair_ref.shape
-    span = pair // 2
-    out_tiles = span // LANES
+    span = out_tiles * LANES
+    newer = jnp.where(chip >= 1, back1_ref[...].astype(jnp.float32), 0.0)
+    every = jnp.concatenate([newer, pair_ref[...].astype(jnp.float32)], axis=1)
+    known = every.shape[1] - span
+    window = jnp.where(second, every[:, span:], every[:, :known])
+    count = known // LANES
+    tiles = [window[:, LANES * t : LANES * (t + 1)] for t in range(count)]
+    for t, rows in enumerate(hankel_rows(tiles, jnp.zeros((SUB, LANES), jnp.float32))):
+        hankel_ref[t] = rows.astype(hankel_ref.dtype)
+    for t in range(count, hankel_ref.shape[0]):
+        hankel_ref[t] = jnp.zeros(hankel_ref.shape[1:], hankel_ref.dtype)
+    first = 2 * out_tiles
+    steps = range(first, toeplitz_ref.shape[1] // LANES, 2)
+    total_ref[...] = banded_product(jnp.zeros(total_ref.shape, jnp.float32), hankel_ref, first, toeplitz_ref, steps, out_tiles)
+
+
+def far_kernel(out_tiles, copies, back2_ref, back1_ref, near_ref, near_hankel_ref, toeplitz_ref, out_ref, hankel):
+    place = lax.axis_index("tm")
+    chip, second = place // 2, lax.rem(place, 2) == 1
+    modes = out_ref.shape[1]
+    span = out_tiles * LANES
     older = jnp.where(chip >= 2, back2_ref[...].astype(jnp.float32), 0.0)
-    newer = jnp.where(chip >= 1, back1_ref[...].astype(jnp.float32), 0.0)
-    every = jnp.concatenate([older, newer, pair_ref[...].astype(jnp.float32)], axis=1)
-    window = span + tap_tiles * LANES
-    window = jnp.where(second, every[:, span : span + window], every[:, :window])
-    count = window.shape[1] // LANES
-    tiles = [window[:, LANES * t : LANES * (t + 1)] for t in range(count)]
+    newer = jnp.where(chip >= 1, back1_ref[:, : span + LANES].astype(jnp.float32), 0.0)
+    every = jnp.concatenate([older, newer], axis=1)
+    first = 2 * out_tiles
+    width = first * LANES + LANES
+    window = jnp.where(second, every[:, span : span + width], every[:, :width])
+    tiles = [window[:, LANES * t : LANES * (t + 1)] for t in range(first)]
+    for t, rows in enumerate(hankel_rows(tiles, window[:, first * LANES :])):
+        hankel[t] = rows.astype(hankel.dtype)
+    hankel[first:] = near_hankel_ref[: hankel.shape[0] - first]
+    total = banded_product(near_ref[...], hankel, 0, toeplitz_ref, range(0, first, 2), out_tiles)
     lane = lax.broadcasted_iota(jnp.int32, (SUB, LANES), 1)
-    zero = jnp.zeros((SUB, LANES), jnp.float32)
-    rolled = [[tile] + [pltpu.roll(tile, LANES - STEP * j, 1) for j in range(1, PER_TILE)] for tile in tiles]
-    rolled.append([zero] * PER_TILE)
-    for t in range(count):
-        rows = [tiles[t]] + [
-            jnp.where(lane < LANES - STEP * j, rolled[t][j], rolled[t + 1][j]) for j in range(1, PER_TILE)
-        ]
-        hankel[t] = jnp.concatenate(rows, axis=0).astype(hankel.dtype)
-    for t in range(count, hankel.shape[0]):
-        hankel[t] = jnp.zeros(hankel.shape[1:], hankel.dtype)
-    depth = toeplitz_ref.shape[1]
-    rows = out_tiles * PER_TILE * modes
-    contract = (((1,), (1,)), ((), ()))
-    total = jnp.zeros((rows, STEP * modes), jnp.float32)
-    for c in range(0, depth // LANES, 2):
-        left = jnp.concatenate(
-            [hankel[c + k : c + k + out_tiles].reshape(rows, LANES) for k in range(2)], axis=1
-        )
-        total = total + lax.dot_general(
-            left, toeplitz_ref[:, LANES * c : LANES * (c + 2)], contract, preferred_element_type=jnp.float32
-        )
     sub = lax.broadcasted_iota(jnp.int32, (SUB, LANES), 0)
     place_in_tile, column = sub % PER_TILE, lane // STEP
     for g in range(out_tiles):
@@ -130,7 +157,7 @@
             for h in range(1, STEP * modes // LANES):
                 own = jnp.where(sub // PER_TILE == h, block[:, LANES * h : LANES * (h + 1)], own)
             picked.append(own)
-        tile = zero
+        tile = jnp.zeros((SUB, LANES), jnp.float32)
         for d in range(PER_TILE):
             line = picked[d]
             for s in range(1, PER_TILE):
@@ -141,6 +168,20 @@
         tile = tile.astype(out_ref.dtype)
         for k in range(copies):
             out_ref[k, :, LANES * g : LANES * (g + 1)] = tile
+
+
+def sag_kernel(responses_ref, modes_ref, out_hbm, blocks_ref, sems):
+    blocks, span = blocks_ref.shape[:2]
+    modes = modes_ref[...]
+    copies = []
+    for k in range(blocks):
+        part = responses_ref[:, :, span * k : span * (k + 1)].reshape(modes.shape[1], span)
+        product = lax.dot_general(part, modes, (((0,), (1,)), ((), ())), preferred_element_type=jnp.float32)
+        blocks_ref[k] = product.astype(blocks_ref.dtype)
+        copies.append(pltpu.make_async_copy(blocks_ref.at[k], out_hbm.at[pl.ds(span * k, span)], sems.at[k]))
+        copies[-1].start()
+    for copy in copies:
+        copy.wait()
 
 
 def on_chip(kernel, shape, dtype, scratch=(), flops=0, bytes_accessed=0):
@@ -178,26 +219,41 @@
     parts = lax.all_to_all(partial, "port", 0, 0, tiled=True)
     tap_tiles = span // LANES
     depth = (tap_tiles + 2) * LANES
-    toeplitz = on_chip(
-        functools.partial(toeplitz_kernel, tap_tiles, depth),
-        (STEP * modes, depth),
-        jnp.bfloat16,
-        flops=2 * 10**9,
-        bytes_accessed=2 * STEP * modes * depth,
-    )(taps)
     pair = on_chip(projection_kernel, (modes, 2 * cycles), jnp.bfloat16)(parts, held, other)
     back2 = lax.ppermute(pair, "tm", [(i, (i + 4) % steps) for i in range(steps)])
     back1 = lax.ppermute(pair, "tm", [(i, (i + 2) % steps) for i in range(steps)])
+    out_tiles = cycles // LANES
+    rows = STEP * modes
+    near, near_hankel, toeplitz = pl.pallas_call(
+        functools.partial(near_kernel, out_tiles),
+        out_shape=(
+            jax.ShapeDtypeStruct((out_tiles * PER_TILE * modes, rows), jnp.float32),
+            jax.ShapeDtypeStruct((tap_tiles + 2 - out_tiles, PER_TILE * modes, LANES), jnp.bfloat16),
+            jax.ShapeDtypeStruct((rows, depth), jnp.bfloat16),
+        ),
+        compiler_params=pltpu.CompilerParams(vmem_limit_bytes=40 * 1024 * 1024),
+        cost_estimate=pl.CostEstimate(flops=2 * 10**9, bytes_accessed=4 * rows * depth, transcendentals=0),
+    )(back1, pair, taps)
     responses = on_chip(
-        functools.partial(convolution_kernel, tap_tiles, ports),
+        functools.partial(far_kernel, out_tiles, ports),
         (ports, modes, cycles),
         jnp.bfloat16,
-        scratch=[pltpu.VMEM((tap_tiles + 1 + cycles // LANES + 1, PER_TILE * modes, LANES), jnp.bfloat16)],
-    )(back2, back1, pair, toeplitz)
-    complete = lax.all_to_all(responses, "port", 0, 0, tiled=True).reshape(ports * modes, cycles)
-    return jnp.einsum("vm,uv->mu", complete, eigen_vectors_at_pins, preferred_element_type=jnp.float32).astype(
-        jnp.bfloat16
-    )
+        scratch=[pltpu.VMEM((3 * out_tiles, PER_TILE * modes, LANES), jnp.bfloat16)],
+    )(back2, back1, near, near_hankel, toeplitz)
+    complete = lax.all_to_all(responses, "port", 0, 0, tiled=True)
+    local_ports = eigen_vectors_at_pins.shape[0]
+    blocks = 4
+    return pl.pallas_call(
+        sag_kernel,
+        out_shape=jax.ShapeDtypeStruct((cycles, local_ports), jnp.bfloat16),
+        in_specs=[in_vmem] * 2,
+        out_specs=pl.BlockSpec(memory_space=pltpu.HBM),
+        scratch_shapes=[
+            pltpu.VMEM((blocks, cycles // blocks, local_ports), jnp.bfloat16),
+            pltpu.SemaphoreType.DMA((blocks,)),
+        ],
+        compiler_params=pltpu.CompilerParams(vmem_limit_bytes=16 * 1024 * 1024),
+    )(complete, eigen_vectors_at_pins)
 
 
 def solution(mesh):

time: 52.5 us -> 52.1 us (level)
  matrix products: 1.15 us -> 0 us
  Pallas kernels: 3.39 us -> 4.45 us
    dot_general x1 -> x0, matrix products: 1.15 us -> none  [per_device(): jnp.einsum('vm,uv->mu', complete, eigen_vectors_at_pins, preferred_elemen...]
    ppermute x1, waiting for transfers between devices: 1.56 us -> 0.47 us  [per_device(): lax.ppermute(pair, 'tm', [(i, (i + 4) % steps) for i in range(steps)])]
    pallas_call x2 -> x3, Pallas kernels: 1.74 us -> 2.8 us  [the longest x1 1.09 us: per_device(): pl.pallas_call(sag_kernel, out_shape=jax.ShapeDtypeStruct((cycles, local_...]
    ppermute x1, waiting for transfers between devices: 0.35 us -> 1.13 us  [per_device(): lax.ppermute(pair, 'tm', [(i, (i + 2) % steps) for i in range(steps)])]
where the time goes in v3:
time: 52.1 us; the launch traced here: 52 us
  blocking collectives  41.6 us (80%)
  Pallas kernels  4.45 us (9%)
  starting transfers between devices  4.29 us (8%)
  waiting for transfers between devices  1.6 us (3%)
    all_to_all x1, blocking collectives, per_device(): parts = lax.all_to_all(partial, 'port', 0, 0, tiled=True)  21.5 us
    all_to_all x1, blocking collectives, per_device(): complete = lax.all_to_all(responses, 'port', 0, 0, tiled=True)  20 us
    ppermute x1, starting transfers between devices, per_device(): lax.ppermute(pair, 'tm', [(i, (i + 4) % steps) for i in range(steps)])  2.73 us
    ppermute x1, starting transfers between devices, per_device(): lax.ppermute(pair, 'tm', [(i, (i + 2) % steps) for i in range(steps)])  1.56 us
    pallas_call x1, Pallas kernels, per_device(): pl.pallas_call(merging_kernel, out_shape=(jax.ShapeDtypeStruct((ports, mo...  1.25 us
    ppermute x1, waiting for transfers between devices, per_device(): lax.ppermute(pair, 'tm', [(i, (i + 2) % steps) for i in range(steps)])  1.13 us
    pallas_call x1, Pallas kernels, per_device(): pl.pallas_call(sag_kernel, out_shape=jax.ShapeDtypeStruct((cycles, local_...  1.09 us
    pallas_call x1, Pallas kernels, per_device(): pl.pallas_call(functools.partial(near_kernel, out_tiles), out_shape=(jax....  1.07 us
  transfers between devices with their start and end apart: 3, of which 2 were waited for; matrix products, arithmetic and copies ran while one was open for 0% of the time, Pallas kernels for 4%

profile of v3, /device:TPU:32, one launch (start us, length us, event | category | flops | bytes accessed | tf_op | source)
XLA Modules:
  0.0 52.0 jit_solution(7328597752156673736)
XLA Ops:
  0.0 0.0 copy-start.1
  0.0 0.0 collective-permute-start
  0.0 1.3 %shard_map.46 = (bf16[32,8,256]{2,1,0:T(8,128)(2,1)S(1)}, bf16[1024,256]{1,0:T(8,128)(2,1)S(1)}) custom-call(bf16[256,256]{1,0:T(8,128)(2,1)} %signatures_hbm.1, bf16[256,256]{1,0:T(8,128)(2,1)} %modes_ref.1, bf16[1024,256]{1,0:T(8,128)(2,1)} %counters_hbm.1), custom_call_target="tpu_custom_call" | custom-call | tf_op jit(solution)/shard_map/pallas_call | solution.py:204
  1.3 21.5 %all_to_all.10.parts_ref = bf16[32,8,256]{2,1,0:T(8,128)(2,1)S(1)} all-to-all(bf16[32,8,256]{2,1,0:T(8,128)(2,1)S(1)} %get-tuple-element.10), channel_id=1, replica_groups=mesh['tm'=8,'port'=32] {'port'}, dimensions={0} | all-to-all | bytes 262144 | tf_op jit(solution)/shard_map/all_to_all | solution.py:219
  22.8 0.0 collective-permute-done.other_ref
  22.8 0.4 shard_map.47.pair_ref
  23.2 1.6 %collective-permute-start.2 = (bf16[8,2048]{1,0:T(8,128)(2,1)S(1)}, bf16[8,2048]{1,0:T(8,128)(2,1)S(1)}, u32[]{:S(2)}, u32[]{:S(2)}) collective-permute-start(bf16[8,2048]{1,0:T(8,128)(2,1)S(1)} %shard_map.47.pair_ref), channel_id=1, source_target_pairs={{0,64},{32,96},{64,128},{96,160},{128,192},{160,224},{192,0},{224,... | collective-permute-start | bytes 98312 | tf_op jit(solution)/shard_map/ppermute | solution.py:224
  24.8 2.7 %collective-permute-start.1 = (bf16[8,2048]{1,0:T(8,128)(2,1)S(1)}, bf16[8,2048]{1,0:T(8,128)(2,1)S(1)}, u32[]{:S(2)}, u32[]{:S(2)}) collective-permute-start(bf16[8,2048]{1,0:T(8,128)(2,1)S(1)} %shard_map.47.pair_ref), channel_id=1, source_target_pairs={{0,128},{32,160},{64,192},{96,224},{128,0},{160,32},{192,64},{224,... | collective-permute-start | bytes 98312 | tf_op jit(solution)/shard_map/ppermute | solution.py:223
  27.5 1.1 %collective-permute-done.2.back1_ref = bf16[8,2048]{1,0:T(8,128)(2,1)S(1)} collective-permute-done((bf16[8,2048]{1,0:T(8,128)(2,1)S(1)}, bf16[8,2048]{1,0:T(8,128)(2,1)S(1)}, u32[]{:S(2)}, u32[]{:S(2)}) %collective-permute-start.2) | collective-permute-done | bytes 32800 | tf_op jit(solution)/shard_map/ppermute | solution.py:224
  28.6 0.0 copy-done.1
  28.6 1.1 %shard_map.48 = (f32[256,256]{1,0:T(8,128)S(1)}, bf16[26,32,128]{2,1,0:T(8,128)(2,1)S(1)}, bf16[256,4352]{1,0:T(8,128)(2,1)S(1)}) custom-call(bf16[8,2048]{1,0:T(8,128)(2,1)S(1)} %collective-permute-done.2.back1_ref, bf16[8,2048]{1,0:T(8,128)(2,1)S(1)} %shard_map.47.pair_ref, bf16[8,4096]{1,0:T(8,128)(2,1)S(1)} %copy-done.1), custom_call_target="tpu_custom_call" | custom-call | flops 2000000000 | bytes 4456448 | tf_op jit(solution)/shard_map/pallas_call | solution.py:227
  29.7 0.0 copy-start
  29.7 0.5 collective-permute-done.1.back2_ref
  30.2 0.6 %shard_map.49 = bf16[32,8,1024]{2,1,0:T(8,128)(2,1)S(1)} custom-call(bf16[8,2048]{1,0:T(8,128)(2,1)S(1)} %collective-permute-done.1.back2_ref, bf16[8,2048]{1,0:T(8,128)(2,1)S(1)} %collective-permute-done.2.back1_ref, f32[256,256]{1,0:T(8,128)S(1)} %get-tuple-element.12.near_ref, bf16[26,32,128]{2,1,0:T(8,128)(2,1)S(1)} %get-tuple-element.13.near_hankel_ref, ...), custom_call_target="tpu_custom_call" | custom-call | tf_op jit(solution)/shard_map/pallas_call | solution.py:237
  30.8 20.0 %all_to_all.11.responses_ref = bf16[32,8,1024]{2,1,0:T(8,128)(2,1)S(1)} all-to-all(bf16[32,8,1024]{2,1,0:T(8,128)(2,1)S(1)} %shard_map.49), channel_id=1, replica_groups=mesh['tm'=8,'port'=32] {'port'}, dimensions={0} | all-to-all | bytes 1048576 | tf_op jit(solution)/shard_map/all_to_all | solution.py:243
  50.9 0.0 copy-done
  50.9 1.1 %shard_map.50 = bf16[1024,256]{1,0:T(8,128)(2,1)} custom-call(bf16[32,8,1024]{2,1,0:T(8,128)(2,1)S(1)} %all_to_all.11.responses_ref, bf16[256,256]{1,0:T(8,128)(2,1)S(1)} %copy-done), custom_call_target="tpu_custom_call" | custom-call | tf_op jit(solution)/shard_map/pallas_call | solution.py:246
Async XLA Ops:
  0.0 28.6 %copy-start.1 = (bf16[8,4096]{1,0:T(8,128)(2,1)S(1)}, bf16[8,4096]{1,0:T(8,128)(2,1)}, u32[]{:S(2)}) copy-start(bf16[8,4096]{1,0:T(8,128)(2,1)} %taps_ref.1) | copy-start | bytes 196612
  0.0 22.8 %collective-permute-start = (bf16[1024,256]{1,0:T(8,128)(2,1)}, bf16[1024,256]{1,0:T(8,128)(2,1)S(1)}, u32[]{:S(2)}, u32[]{:S(2)}) collective-permute-start(bf16[1024,256]{1,0:T(8,128)(2,1)} %counters_hbm.1), channel_id=1, source_target_pairs={{0,32},{32,0},{64,96},{96,64},{128,160},{160,128},{192,224},{224,1... | collective-permute-start | bytes 1572872 | tf_op jit(solution)/shard_map/ppermute | solution.py:201
  23.2 5.4 %collective-permute-start.2 = (bf16[8,2048]{1,0:T(8,128)(2,1)S(1)}, bf16[8,2048]{1,0:T(8,128)(2,1)S(1)}, u32[]{:S(2)}, u32[]{:S(2)}) collective-permute-start(bf16[8,2048]{1,0:T(8,128)(2,1)S(1)} %shard_map.47.pair_ref), channel_id=1, source_target_pairs={{0,64},{32,96},{64,128},{96,160},{128,192},{160,224},{192,0},{224,... | collective-permute-start | bytes 98312 | tf_op jit(solution)/shard_map/ppermute | solution.py:224
  24.8 5.4 %collective-permute-start.1 = (bf16[8,2048]{1,0:T(8,128)(2,1)S(1)}, bf16[8,2048]{1,0:T(8,128)(2,1)S(1)}, u32[]{:S(2)}, u32[]{:S(2)}) collective-permute-start(bf16[8,2048]{1,0:T(8,128)(2,1)S(1)} %shard_map.47.pair_ref), channel_id=1, source_target_pairs={{0,128},{32,160},{64,192},{96,224},{128,0},{160,32},{192,64},{224,... | collective-permute-start | bytes 98312 | tf_op jit(solution)/shard_map/ppermute | solution.py:223
  29.7 21.2 %copy-start = (bf16[256,256]{1,0:T(8,128)(2,1)S(1)}, bf16[256,256]{1,0:T(8,128)(2,1)}, u32[]{:S(2)}) copy-start(bf16[256,256]{1,0:T(8,128)(2,1)} %modes_ref.1) | copy-start | bytes 393220

commit v4 on v3

--- a/solution.py
+++ b/solution.py
@@ -46,21 +46,45 @@
             before = now
 
 
-def merging_kernel(signatures_hbm, modes_hbm, counters_hbm, partial_ref, counters_ref, signatures_ref, modes_ref, sems):
+def is_second():
+    return lax.rem(lax.axis_index("tm"), 2) == 1
+
+
+def merging_kernel(
+    signatures_hbm,
+    modes_hbm,
+    counters_hbm,
+    taps_hbm,
+    partial_ref,
+    counters_ref,
+    toeplitz_ref,
+    signatures_ref,
+    modes_ref,
+    taps_ref,
+    sems,
+):
     copies = [
         pltpu.make_async_copy(signatures_hbm, signatures_ref, sems.at[0]),
         pltpu.make_async_copy(modes_hbm, modes_ref, sems.at[1]),
-        pltpu.make_async_copy(counters_hbm, counters_ref, sems.at[2]),
+        pltpu.make_async_copy(taps_hbm, taps_ref, sems.at[2]),
+        pltpu.make_async_copy(counters_hbm, counters_ref, sems.at[3]),
     ]
     for copy in copies:
         copy.start()
+    copies[2].wait()
+
+    @pl.when(jnp.logical_not(is_second()))
+    def _():
+        fill_toeplitz(taps_ref.shape[1] // LANES, toeplitz_ref.shape[1], taps_ref, toeplitz_ref)
+
     copies[0].wait()
     copies[1].wait()
     partial = lax.dot_general(
         modes_ref[...], signatures_ref[...], (((0,), (1,)), ((), ())), preferred_element_type=jnp.float32
     )
     partial_ref[...] = partial.reshape(partial_ref.shape).astype(partial_ref.dtype)
-    copies[2].wait()
+
+    copies[3].wait()
 
 
 def projection_kernel(parts_ref, own_ref, other_ref, out_ref):
@@ -78,7 +102,7 @@
         return terms[:modes] + (terms[modes : 2 * modes] + terms[2 * modes : 3 * modes])
 
     own, other = modal(own_ref), modal(other_ref)
-    first = lax.rem(lax.axis_index("tm"), 2) == 0
+    first = jnp.logical_not(is_second())
     span = own.shape[1]
     out_ref[:, :span] = jnp.where(first, own, other).astype(out_ref.dtype)
     out_ref[:, span:] = jnp.where(first, other, own).astype(out_ref.dtype)
@@ -109,8 +133,13 @@
     return total
 
 
-def near_kernel(out_tiles, back1_ref, pair_ref, taps_ref, total_ref, hankel_ref, toeplitz_ref):
-    fill_toeplitz(taps_ref.shape[1] // LANES, toeplitz_ref.shape[1], taps_ref, toeplitz_ref)
+def near_kernel(out_tiles, back1_ref, pair_ref, taps_ref, formed_ref, total_ref, hankel_ref, toeplitz_ref):
+    del formed_ref
+
+    @pl.when(is_second())
+    def _():
+        fill_toeplitz(taps_ref.shape[1] // LANES, toeplitz_ref.shape[1], taps_ref, toeplitz_ref)
+
     place = lax.axis_index("tm")
     chip, second = place // 2, lax.rem(place, 2) == 1
     span = out_tiles * LANES
@@ -201,24 +230,26 @@
     other = lax.ppermute(counters, "tm", swap)
     in_hbm = pl.BlockSpec(memory_space=pltpu.HBM)
     in_vmem = pl.BlockSpec(memory_space=pltpu.VMEM)
-    partial, held = pl.pallas_call(
+    depth = span + 2 * LANES
+    partial, held, formed = pl.pallas_call(
         merging_kernel,
         out_shape=(
             jax.ShapeDtypeStruct((ports, modes, tallies), jnp.bfloat16),
             jax.ShapeDtypeStruct(counters.shape, counters.dtype),
+            jax.ShapeDtypeStruct((STEP * modes, depth), jnp.bfloat16),
         ),
-        in_specs=[in_hbm] * 3,
-        out_specs=(in_vmem, in_vmem),
+        in_specs=[in_hbm] * 4,
+        out_specs=(in_vmem,) * 3,
         scratch_shapes=[
             pltpu.VMEM(signatures.shape, signatures.dtype),
             pltpu.VMEM(eigen_vectors_at_pins.shape, eigen_vectors_at_pins.dtype),
-            pltpu.SemaphoreType.DMA((3,)),
+            pltpu.VMEM(taps.shape, taps.dtype),
+            pltpu.SemaphoreType.DMA((4,)),
         ],
         compiler_params=pltpu.CompilerParams(vmem_limit_bytes=16 * 1024 * 1024),
-    )(*[pltpu.with_memory_space_constraint(x, pltpu.HBM) for x in (signatures, eigen_vectors_at_pins, counters)])
+    )(*[pltpu.with_memory_space_constraint(x, pltpu.HBM) for x in (signatures, eigen_vectors_at_pins, counters, taps)])
     parts = lax.all_to_all(partial, "port", 0, 0, tiled=True)
     tap_tiles = span // LANES
-    depth = (tap_tiles + 2) * LANES
     pair = on_chip(projection_kernel, (modes, 2 * cycles), jnp.bfloat16)(parts, held, other)
     back2 = lax.ppermute(pair, "tm", [(i, (i + 4) % steps) for i in range(steps)])
     back1 = lax.ppermute(pair, "tm", [(i, (i + 2) % steps) for i in range(steps)])
@@ -231,9 +262,10 @@
             jax.ShapeDtypeStruct((tap_tiles + 2 - out_tiles, PER_TILE * modes, LANES), jnp.bfloat16),
             jax.ShapeDtypeStruct((rows, depth), jnp.bfloat16),
         ),
+        input_output_aliases={3: 2},
         compiler_params=pltpu.CompilerParams(vmem_limit_bytes=40 * 1024 * 1024),
         cost_estimate=pl.CostEstimate(flops=2 * 10**9, bytes_accessed=4 * rows * depth, transcendentals=0),
-    )(back1, pair, taps)
+    )(back1, pair, taps, formed)
     responses = on_chip(
         functools.partial(far_kernel, out_tiles, ports),
         (ports, modes, cycles),

time: 52.1 us -> 51.3 us (0.985)
  blocking collectives: 41.6 us -> 39.9 us
  waiting for transfers between devices: 1.6 us -> 2.14 us
    all_to_all x1, blocking collectives: 20 us -> 19 us  [per_device(): complete = lax.all_to_all(responses, 'port', 0, 0, tiled=True)]
    ppermute x1, waiting for transfers between devices: 0.47 us -> 1.24 us  [per_device(): lax.ppermute(pair, 'tm', [(i, (i + 4) % steps) for i in range(steps)])]
    pallas_call x1, Pallas kernels: 1.25 us -> 2.02 us  [per_device(): pl.pallas_call(merging_kernel, out_shape=(jax.ShapeDtypeStruct((ports, mo...]
    all_to_all x1, blocking collectives: 21.5 us -> 20.9 us  [per_device(): parts = lax.all_to_all(partial, 'port', 0, 0, tiled=True)]
    pallas_call x1, Pallas kernels: 1.07 us -> 0.52 us  [per_device(): pl.pallas_call(functools.partial(near_kernel, out_tiles), out_shape=(jax....]
  transfers between devices with their start and end apart: 3 -> 3, of which waited for: 2 -> 2; matrix products, arithmetic and copies ran while one was open for 0% -> 0% of each run, Pallas kernels for 4% -> 5%
where the time goes in v4:
time: 51.3 us; the launch traced here: 51.1 us
  blocking collectives  39.9 us (78%)
  Pallas kernels  4.67 us (9%)
  starting transfers between devices  4.29 us (8%)
  waiting for transfers between devices  2.14 us (4%)
    all_to_all x1, blocking collectives, per_device(): parts = lax.all_to_all(partial, 'port', 0, 0, tiled=True)  20.9 us
    all_to_all x1, blocking collectives, per_device(): complete = lax.all_to_all(responses, 'port', 0, 0, tiled=True)  19 us
    ppermute x1, starting transfers between devices, per_device(): lax.ppermute(pair, 'tm', [(i, (i + 4) % steps) for i in range(steps)])  2.73 us
    pallas_call x1, Pallas kernels, per_device(): pl.pallas_call(merging_kernel, out_shape=(jax.ShapeDtypeStruct((ports, mo...  2.02 us
    ppermute x1, starting transfers between devices, per_device(): lax.ppermute(pair, 'tm', [(i, (i + 2) % steps) for i in range(steps)])  1.56 us
    ppermute x1, waiting for transfers between devices, per_device(): lax.ppermute(pair, 'tm', [(i, (i + 4) % steps) for i in range(steps)])  1.24 us
    pallas_call x1, Pallas kernels, per_device(): pl.pallas_call(sag_kernel, out_shape=jax.ShapeDtypeStruct((cycles, local_...  1.09 us
  transfers between devices with their start and end apart: 3, of which 2 were waited for; matrix products, arithmetic and copies ran while one was open for 0% of the time, Pallas kernels for 5%

profile of v4, /device:TPU:32, one launch (start us, length us, event | category | flops | bytes accessed | tf_op | source)
XLA Modules:
  0.0 51.1 jit_solution(7328077510683195949)
XLA Ops:
  0.0 0.0 copy-start.1
  0.0 0.0 collective-permute-start
  0.0 2.0 %shard_map.46 = (bf16[32,8,256]{2,1,0:T(8,128)(2,1)S(1)}, bf16[1024,256]{1,0:T(8,128)(2,1)S(1)}, bf16[256,4352]{1,0:T(8,128)(2,1)S(1)}) custom-call(bf16[256,256]{1,0:T(8,128)(2,1)} %signatures_hbm.1, bf16[256,256]{1,0:T(8,128)(2,1)} %modes_ref.1, bf16[1024,256]{1,0:T(8,128)(2,1)} %counters_hbm.1, bf16[8,4096]{1,0:T(8,128)(2,1)} %taps_ref.1), custom_call_target="tpu_custom_call" | custom-call | tf_op jit(solution)/shard_map/pallas_call | solution.py:234
  2.0 20.9 %all_to_all.10.parts_ref = bf16[32,8,256]{2,1,0:T(8,128)(2,1)S(1)} all-to-all(bf16[32,8,256]{2,1,0:T(8,128)(2,1)S(1)} %get-tuple-element.11), channel_id=1, replica_groups=mesh['tm'=8,'port'=32] {'port'}, dimensions={0} | all-to-all | bytes 262144 | tf_op jit(solution)/shard_map/all_to_all | solution.py:251
  22.9 0.0 collective-permute-done.other_ref
  22.9 0.4 shard_map.47.pair_ref
  23.3 1.6 %collective-permute-start.2 = (bf16[8,2048]{1,0:T(8,128)(2,1)S(1)}, bf16[8,2048]{1,0:T(8,128)(2,1)S(1)}, u32[]{:S(2)}, u32[]{:S(2)}) collective-permute-start(bf16[8,2048]{1,0:T(8,128)(2,1)S(1)} %shard_map.47.pair_ref), channel_id=1, source_target_pairs={{0,64},{32,96},{64,128},{96,160},{128,192},{160,224},{192,0},{224,... | collective-permute-start | bytes 98312 | tf_op jit(solution)/shard_map/ppermute | solution.py:255
  24.9 2.7 %collective-permute-start.1 = (bf16[8,2048]{1,0:T(8,128)(2,1)S(1)}, bf16[8,2048]{1,0:T(8,128)(2,1)S(1)}, u32[]{:S(2)}, u32[]{:S(2)}) collective-permute-start(bf16[8,2048]{1,0:T(8,128)(2,1)S(1)} %shard_map.47.pair_ref), channel_id=1, source_target_pairs={{0,128},{32,160},{64,192},{96,224},{128,0},{160,32},{192,64},{224,... | collective-permute-start | bytes 98312 | tf_op jit(solution)/shard_map/ppermute | solution.py:254
  27.6 0.9 %collective-permute-done.2.back1_ref = bf16[8,2048]{1,0:T(8,128)(2,1)S(1)} collective-permute-done((bf16[8,2048]{1,0:T(8,128)(2,1)S(1)}, bf16[8,2048]{1,0:T(8,128)(2,1)S(1)}, u32[]{:S(2)}, u32[]{:S(2)}) %collective-permute-start.2) | collective-permute-done | bytes 32800 | tf_op jit(solution)/shard_map/ppermute | solution.py:255
  28.5 0.0 copy-done.1
  28.5 0.5 %shard_map.48 = (f32[256,256]{1,0:T(8,128)S(1)}, bf16[26,32,128]{2,1,0:T(8,128)(2,1)S(1)}, bf16[256,4352]{1,0:T(8,128)(2,1)S(1)}) custom-call(bf16[8,2048]{1,0:T(8,128)(2,1)S(1)} %collective-permute-done.2.back1_ref, bf16[8,2048]{1,0:T(8,128)(2,1)S(1)} %shard_map.47.pair_ref, bf16[8,4096]{1,0:T(8,128)(2,1)S(1)} %copy-done.1, ...), custom_call_target="tpu_custom_call", output_to_operand_aliasing={{2}: (3, {})} | custom-call | flops 2000000000 | bytes 4456448 | tf_op jit(solution)/shard_map/pallas_call | solution.py:258
  29.0 0.0 copy-start
  29.1 1.2 %collective-permute-done.1.back2_ref = bf16[8,2048]{1,0:T(8,128)(2,1)S(1)} collective-permute-done((bf16[8,2048]{1,0:T(8,128)(2,1)S(1)}, bf16[8,2048]{1,0:T(8,128)(2,1)S(1)}, u32[]{:S(2)}, u32[]{:S(2)}) %collective-permute-start.1) | collective-permute-done | bytes 32800 | tf_op jit(solution)/shard_map/ppermute | solution.py:254
  30.3 0.6 %shard_map.49 = bf16[32,8,1024]{2,1,0:T(8,128)(2,1)S(1)} custom-call(bf16[8,2048]{1,0:T(8,128)(2,1)S(1)} %collective-permute-done.1.back2_ref, bf16[8,2048]{1,0:T(8,128)(2,1)S(1)} %collective-permute-done.2.back1_ref, f32[256,256]{1,0:T(8,128)S(1)} %get-tuple-element.14.near_ref, bf16[26,32,128]{2,1,0:T(8,128)(2,1)S(1)} %get-tuple-element.15.near_hankel_ref, ...), custom_call_target="tpu_custom_call" | custom-call | tf_op jit(solution)/shard_map/pallas_call | solution.py:269
  30.9 19.0 %all_to_all.11.responses_ref = bf16[32,8,1024]{2,1,0:T(8,128)(2,1)S(1)} all-to-all(bf16[32,8,1024]{2,1,0:T(8,128)(2,1)S(1)} %shard_map.49), channel_id=1, replica_groups=mesh['tm'=8,'port'=32] {'port'}, dimensions={0} | all-to-all | bytes 1048576 | tf_op jit(solution)/shard_map/all_to_all | solution.py:275
  50.0 0.0 copy-done
  50.0 1.1 %shard_map.50 = bf16[1024,256]{1,0:T(8,128)(2,1)} custom-call(bf16[32,8,1024]{2,1,0:T(8,128)(2,1)S(1)} %all_to_all.11.responses_ref, bf16[256,256]{1,0:T(8,128)(2,1)S(1)} %copy-done), custom_call_target="tpu_custom_call" | custom-call | tf_op jit(solution)/shard_map/pallas_call | solution.py:278
Async XLA Ops:
  0.0 28.5 %copy-start.1 = (bf16[8,4096]{1,0:T(8,128)(2,1)S(1)}, bf16[8,4096]{1,0:T(8,128)(2,1)}, u32[]{:S(2)}) copy-start(bf16[8,4096]{1,0:T(8,128)(2,1)} %taps_ref.1) | copy-start | bytes 196612
  0.0 22.9 %collective-permute-start = (bf16[1024,256]{1,0:T(8,128)(2,1)}, bf16[1024,256]{1,0:T(8,128)(2,1)S(1)}, u32[]{:S(2)}, u32[]{:S(2)}) collective-permute-start(bf16[1024,256]{1,0:T(8,128)(2,1)} %counters_hbm.1), channel_id=1, source_target_pairs={{0,32},{32,0},{64,96},{96,64},{128,160},{160,128},{192,224},{224,1... | collective-permute-start | bytes 1572872 | tf_op jit(solution)/shard_map/ppermute | solution.py:230
  23.3 5.2 %collective-permute-start.2 = (bf16[8,2048]{1,0:T(8,128)(2,1)S(1)}, bf16[8,2048]{1,0:T(8,128)(2,1)S(1)}, u32[]{:S(2)}, u32[]{:S(2)}) collective-permute-start(bf16[8,2048]{1,0:T(8,128)(2,1)S(1)} %shard_map.47.pair_ref), channel_id=1, source_target_pairs={{0,64},{32,96},{64,128},{96,160},{128,192},{160,224},{192,0},{224,... | collective-permute-start | bytes 98312 | tf_op jit(solution)/shard_map/ppermute | solution.py:255
  24.9 5.4 %collective-permute-start.1 = (bf16[8,2048]{1,0:T(8,128)(2,1)S(1)}, bf16[8,2048]{1,0:T(8,128)(2,1)S(1)}, u32[]{:S(2)}, u32[]{:S(2)}) collective-permute-start(bf16[8,2048]{1,0:T(8,128)(2,1)S(1)} %shard_map.47.pair_ref), channel_id=1, source_target_pairs={{0,128},{32,160},{64,192},{96,224},{128,0},{160,32},{192,64},{224,... | collective-permute-start | bytes 98312 | tf_op jit(solution)/shard_map/ppermute | solution.py:254
  29.0 20.9 %copy-start = (bf16[256,256]{1,0:T(8,128)(2,1)S(1)}, bf16[256,256]{1,0:T(8,128)(2,1)}, u32[]{:S(2)}) copy-start(bf16[256,256]{1,0:T(8,128)(2,1)} %modes_ref.1) | copy-start | bytes 393220

commit v5 on v4

--- a/solution.py
+++ b/solution.py
@@ -140,40 +140,44 @@
     def _():
         fill_toeplitz(taps_ref.shape[1] // LANES, toeplitz_ref.shape[1], taps_ref, toeplitz_ref)
 
-    place = lax.axis_index("tm")
-    chip, second = place // 2, lax.rem(place, 2) == 1
-    span = out_tiles * LANES
+    chip = lax.axis_index("tm") // 2
     newer = jnp.where(chip >= 1, back1_ref[...].astype(jnp.float32), 0.0)
     every = jnp.concatenate([newer, pair_ref[...].astype(jnp.float32)], axis=1)
-    known = every.shape[1] - span
-    window = jnp.where(second, every[:, span:], every[:, :known])
-    count = known // LANES
-    tiles = [window[:, LANES * t : LANES * (t + 1)] for t in range(count)]
-    for t, rows in enumerate(hankel_rows(tiles, jnp.zeros((SUB, LANES), jnp.float32))):
-        hankel_ref[t] = rows.astype(hankel_ref.dtype)
-    for t in range(count, hankel_ref.shape[0]):
-        hankel_ref[t] = jnp.zeros(hankel_ref.shape[1:], hankel_ref.dtype)
-    first = 2 * out_tiles
-    steps = range(first, toeplitz_ref.shape[1] // LANES, 2)
-    total_ref[...] = banded_product(jnp.zeros(total_ref.shape, jnp.float32), hankel_ref, first, toeplitz_ref, steps, out_tiles)
-
-
-def far_kernel(out_tiles, copies, back2_ref, back1_ref, near_ref, near_hankel_ref, toeplitz_ref, out_ref, hankel):
-    place = lax.axis_index("tm")
-    chip, second = place // 2, lax.rem(place, 2) == 1
+
+    def give(first):
+        count = toeplitz_ref.shape[1] // LANES + out_tiles - 2 - first
+        tiles = [every[:, LANES * t : LANES * (t + 1)] for t in range(count)]
+        for t, rows in enumerate(hankel_rows(tiles, jnp.zeros((SUB, LANES), jnp.float32))):
+            hankel_ref[first - out_tiles + t] = rows.astype(hankel_ref.dtype)
+        for t in range(first - out_tiles + count, hankel_ref.shape[0]):
+            hankel_ref[t] = jnp.zeros(hankel_ref.shape[1:], hankel_ref.dtype)
+        steps = range(first, toeplitz_ref.shape[1] // LANES, 2)
+        nothing = jnp.zeros(total_ref.shape, jnp.float32)
+        total_ref[...] = banded_product(nothing, hankel_ref, out_tiles, toeplitz_ref, steps, out_tiles)
+
+    pl.when(is_second())(lambda: give(out_tiles))
+    pl.when(jnp.logical_not(is_second()))(lambda: give(2 * out_tiles))
+
+
+def far_kernel(
+    out_tiles, copies, back2_ref, back1_ref, near_ref, near_hankel_ref, toeplitz_ref, out_ref, hankel, total_ref
+):
+    chip = lax.axis_index("tm") // 2
     modes = out_ref.shape[1]
-    span = out_tiles * LANES
     older = jnp.where(chip >= 2, back2_ref[...].astype(jnp.float32), 0.0)
-    newer = jnp.where(chip >= 1, back1_ref[:, : span + LANES].astype(jnp.float32), 0.0)
-    every = jnp.concatenate([older, newer], axis=1)
-    first = 2 * out_tiles
-    width = first * LANES + LANES
-    window = jnp.where(second, every[:, span : span + width], every[:, :width])
-    tiles = [window[:, LANES * t : LANES * (t + 1)] for t in range(first)]
-    for t, rows in enumerate(hankel_rows(tiles, window[:, first * LANES :])):
-        hankel[t] = rows.astype(hankel.dtype)
-    hankel[first:] = near_hankel_ref[: hankel.shape[0] - first]
-    total = banded_product(near_ref[...], hankel, 0, toeplitz_ref, range(0, first, 2), out_tiles)
+    following = jnp.where(chip >= 1, back1_ref[:, :LANES].astype(jnp.float32), 0.0)
+
+    def add(first):
+        start = 2 * out_tiles - first
+        tiles = [older[:, LANES * t : LANES * (t + 1)] for t in range(start, 2 * out_tiles)]
+        for t, rows in enumerate(hankel_rows(tiles, following)):
+            hankel[t] = rows.astype(hankel.dtype)
+        hankel[first : first + out_tiles] = near_hankel_ref[first - out_tiles : first]
+        total_ref[...] = banded_product(near_ref[...], hankel, 0, toeplitz_ref, range(0, first, 2), out_tiles)
+
+    pl.when(is_second())(lambda: add(out_tiles))
+    pl.when(jnp.logical_not(is_second()))(lambda: add(2 * out_tiles))
+    total = total_ref[...]
     lane = lax.broadcasted_iota(jnp.int32, (SUB, LANES), 1)
     sub = lax.broadcasted_iota(jnp.int32, (SUB, LANES), 0)
     place_in_tile, column = sub % PER_TILE, lane // STEP
@@ -259,7 +263,7 @@
         functools.partial(near_kernel, out_tiles),
         out_shape=(
             jax.ShapeDtypeStruct((out_tiles * PER_TILE * modes, rows), jnp.float32),
-            jax.ShapeDtypeStruct((tap_tiles + 2 - out_tiles, PER_TILE * modes, LANES), jnp.bfloat16),
+            jax.ShapeDtypeStruct((tap_tiles + 2, PER_TILE * modes, LANES), jnp.bfloat16),
             jax.ShapeDtypeStruct((rows, depth), jnp.bfloat16),
         ),
         input_output_aliases={3: 2},
@@ -270,7 +274,10 @@
         functools.partial(far_kernel, out_tiles, ports),
         (ports, modes, cycles),
         jnp.bfloat16,
-        scratch=[pltpu.VMEM((3 * out_tiles, PER_TILE * modes, LANES), jnp.bfloat16)],
+        scratch=[
+            pltpu.VMEM((3 * out_tiles, PER_TILE * modes, LANES), jnp.bfloat16),
+            pltpu.VMEM((out_tiles * PER_TILE * modes, rows), jnp.float32),
+        ],
     )(back2, back1, near, near_hankel, toeplitz)
     complete = lax.all_to_all(responses, "port", 0, 0, tiled=True)
     local_ports = eigen_vectors_at_pins.shape[0]

time: 51.3 us -> 51.4 us (level)
  no operation moved by 1% of the time
where the time goes in v5:
time: 51.4 us; the launch traced here: 51.2 us
  blocking collectives  40 us (78%)
  Pallas kernels  4.73 us (9%)
  starting transfers between devices  4.29 us (8%)
  waiting for transfers between devices  2.14 us (4%)
    all_to_all x1, blocking collectives, per_device(): parts = lax.all_to_all(partial, 'port', 0, 0, tiled=True)  20.9 us
    all_to_all x1, blocking collectives, per_device(): complete = lax.all_to_all(responses, 'port', 0, 0, tiled=True)  19.1 us
    ppermute x1, starting transfers between devices, per_device(): lax.ppermute(pair, 'tm', [(i, (i + 4) % steps) for i in range(steps)])  2.73 us
    pallas_call x1, Pallas kernels, per_device(): pl.pallas_call(merging_kernel, out_shape=(jax.ShapeDtypeStruct((ports, mo...  2.02 us
    ppermute x1, starting transfers between devices, per_device(): lax.ppermute(pair, 'tm', [(i, (i + 2) % steps) for i in range(steps)])  1.56 us
    ppermute x1, waiting for transfers between devices, per_device(): lax.ppermute(pair, 'tm', [(i, (i + 4) % steps) for i in range(steps)])  1.23 us
    pallas_call x1, Pallas kernels, per_device(): pl.pallas_call(sag_kernel, out_shape=jax.ShapeDtypeStruct((cycles, local_...  1.09 us
  transfers between devices with their start and end apart: 3, of which 2 were waited for; matrix products, arithmetic and copies ran while one was open for 0% of the time, Pallas kernels for 5%

profile of v5, /device:TPU:32, one launch (start us, length us, event | category | flops | bytes accessed | tf_op | source)
XLA Modules:
  0.0 51.2 jit_solution(12219194536902202872)
XLA Ops:
  0.0 0.0 copy-start.1
  0.0 0.0 collective-permute-start
  0.0 2.0 %shard_map.46 = (bf16[32,8,256]{2,1,0:T(8,128)(2,1)S(1)}, bf16[1024,256]{1,0:T(8,128)(2,1)S(1)}, bf16[256,4352]{1,0:T(8,128)(2,1)S(1)}) custom-call(bf16[256,256]{1,0:T(8,128)(2,1)} %signatures_hbm.1, bf16[256,256]{1,0:T(8,128)(2,1)} %modes_ref.1, bf16[1024,256]{1,0:T(8,128)(2,1)} %counters_hbm.1, bf16[8,4096]{1,0:T(8,128)(2,1)} %taps_ref.1), custom_call_target="tpu_custom_call" | custom-call | tf_op jit(solution)/shard_map/pallas_call | solution.py:238
  2.0 20.9 %all_to_all.10.parts_ref = bf16[32,8,256]{2,1,0:T(8,128)(2,1)S(1)} all-to-all(bf16[32,8,256]{2,1,0:T(8,128)(2,1)S(1)} %get-tuple-element.11), channel_id=1, replica_groups=mesh['tm'=8,'port'=32] {'port'}, dimensions={0} | all-to-all | bytes 262144 | tf_op jit(solution)/shard_map/all_to_all | solution.py:255
  22.9 0.0 collective-permute-done.other_ref
  22.9 0.4 shard_map.47.pair_ref
  23.3 1.6 %collective-permute-start.2 = (bf16[8,2048]{1,0:T(8,128)(2,1)S(1)}, bf16[8,2048]{1,0:T(8,128)(2,1)S(1)}, u32[]{:S(2)}, u32[]{:S(2)}) collective-permute-start(bf16[8,2048]{1,0:T(8,128)(2,1)S(1)} %shard_map.47.pair_ref), channel_id=1, source_target_pairs={{0,64},{32,96},{64,128},{96,160},{128,192},{160,224},{192,0},{224,... | collective-permute-start | bytes 98312 | tf_op jit(solution)/shard_map/ppermute | solution.py:259
  24.9 2.7 %collective-permute-start.1 = (bf16[8,2048]{1,0:T(8,128)(2,1)S(1)}, bf16[8,2048]{1,0:T(8,128)(2,1)S(1)}, u32[]{:S(2)}, u32[]{:S(2)}) collective-permute-start(bf16[8,2048]{1,0:T(8,128)(2,1)S(1)} %shard_map.47.pair_ref), channel_id=1, source_target_pairs={{0,128},{32,160},{64,192},{96,224},{128,0},{160,32},{192,64},{224,... | collective-permute-start | bytes 98312 | tf_op jit(solution)/shard_map/ppermute | solution.py:258
  27.6 0.9 %collective-permute-done.2.back1_ref = bf16[8,2048]{1,0:T(8,128)(2,1)S(1)} collective-permute-done((bf16[8,2048]{1,0:T(8,128)(2,1)S(1)}, bf16[8,2048]{1,0:T(8,128)(2,1)S(1)}, u32[]{:S(2)}, u32[]{:S(2)}) %collective-permute-start.2) | collective-permute-done | bytes 32800 | tf_op jit(solution)/shard_map/ppermute | solution.py:259
  28.5 0.0 copy-done.1
  28.5 0.5 %shard_map.48 = (f32[256,256]{1,0:T(8,128)S(1)}, bf16[34,32,128]{2,1,0:T(8,128)(2,1)S(1)}, bf16[256,4352]{1,0:T(8,128)(2,1)S(1)}) custom-call(bf16[8,2048]{1,0:T(8,128)(2,1)S(1)} %collective-permute-done.2.back1_ref, bf16[8,2048]{1,0:T(8,128)(2,1)S(1)} %shard_map.47.pair_ref, bf16[8,4096]{1,0:T(8,128)(2,1)S(1)} %copy-done.1, ...), custom_call_target="tpu_custom_call", output_to_operand_aliasing={{2}: (3, {})} | custom-call | flops 2000000000 | bytes 4456448 | tf_op jit(solution)/shard_map/pallas_call | solution.py:262
  29.1 0.0 copy-start
  29.1 1.2 %collective-permute-done.1.back2_ref = bf16[8,2048]{1,0:T(8,128)(2,1)S(1)} collective-permute-done((bf16[8,2048]{1,0:T(8,128)(2,1)S(1)}, bf16[8,2048]{1,0:T(8,128)(2,1)S(1)}, u32[]{:S(2)}, u32[]{:S(2)}) %collective-permute-start.1) | collective-permute-done | bytes 32800 | tf_op jit(solution)/shard_map/ppermute | solution.py:258
  30.3 0.7 %shard_map.49 = bf16[32,8,1024]{2,1,0:T(8,128)(2,1)S(1)} custom-call(bf16[8,2048]{1,0:T(8,128)(2,1)S(1)} %collective-permute-done.1.back2_ref, bf16[8,2048]{1,0:T(8,128)(2,1)S(1)} %collective-permute-done.2.back1_ref, f32[256,256]{1,0:T(8,128)S(1)} %get-tuple-element.14.near_ref, bf16[34,32,128]{2,1,0:T(8,128)(2,1)S(1)} %get-tuple-element.15.near_hankel_ref, ...), custom_call_target="tpu_custom_call" | custom-call | tf_op jit(solution)/shard_map/pallas_call | solution.py:273
  31.0 19.1 %all_to_all.11.responses_ref = bf16[32,8,1024]{2,1,0:T(8,128)(2,1)S(1)} all-to-all(bf16[32,8,1024]{2,1,0:T(8,128)(2,1)S(1)} %shard_map.49), channel_id=1, replica_groups=mesh['tm'=8,'port'=32] {'port'}, dimensions={0} | all-to-all | bytes 1048576 | tf_op jit(solution)/shard_map/all_to_all | solution.py:282
  50.1 0.0 copy-done
  50.1 1.1 %shard_map.50 = bf16[1024,256]{1,0:T(8,128)(2,1)} custom-call(bf16[32,8,1024]{2,1,0:T(8,128)(2,1)S(1)} %all_to_all.11.responses_ref, bf16[256,256]{1,0:T(8,128)(2,1)S(1)} %copy-done), custom_call_target="tpu_custom_call" | custom-call | tf_op jit(solution)/shard_map/pallas_call | solution.py:285
Async XLA Ops:
  0.0 28.5 %copy-start.1 = (bf16[8,4096]{1,0:T(8,128)(2,1)S(1)}, bf16[8,4096]{1,0:T(8,128)(2,1)}, u32[]{:S(2)}) copy-start(bf16[8,4096]{1,0:T(8,128)(2,1)} %taps_ref.1) | copy-start | bytes 196612
  0.0 22.9 %collective-permute-start = (bf16[1024,256]{1,0:T(8,128)(2,1)}, bf16[1024,256]{1,0:T(8,128)(2,1)S(1)}, u32[]{:S(2)}, u32[]{:S(2)}) collective-permute-start(bf16[1024,256]{1,0:T(8,128)(2,1)} %counters_hbm.1), channel_id=1, source_target_pairs={{0,32},{32,0},{64,96},{96,64},{128,160},{160,128},{192,224},{224,1... | collective-permute-start | bytes 1572872 | tf_op jit(solution)/shard_map/ppermute | solution.py:234
  23.3 5.2 %collective-permute-start.2 = (bf16[8,2048]{1,0:T(8,128)(2,1)S(1)}, bf16[8,2048]{1,0:T(8,128)(2,1)S(1)}, u32[]{:S(2)}, u32[]{:S(2)}) collective-permute-start(bf16[8,2048]{1,0:T(8,128)(2,1)S(1)} %shard_map.47.pair_ref), channel_id=1, source_target_pairs={{0,64},{32,96},{64,128},{96,160},{128,192},{160,224},{192,0},{224,... | collective-permute-start | bytes 98312 | tf_op jit(solution)/shard_map/ppermute | solution.py:259
  24.9 5.4 %collective-permute-start.1 = (bf16[8,2048]{1,0:T(8,128)(2,1)S(1)}, bf16[8,2048]{1,0:T(8,128)(2,1)S(1)}, u32[]{:S(2)}, u32[]{:S(2)}) collective-permute-start(bf16[8,2048]{1,0:T(8,128)(2,1)S(1)} %shard_map.47.pair_ref), channel_id=1, source_target_pairs={{0,128},{32,160},{64,192},{96,224},{128,0},{160,32},{192,64},{224,... | collective-permute-start | bytes 98312 | tf_op jit(solution)/shard_map/ppermute | solution.py:258
  29.1 21.0 %copy-start = (bf16[256,256]{1,0:T(8,128)(2,1)S(1)}, bf16[256,256]{1,0:T(8,128)(2,1)}, u32[]{:S(2)}) copy-start(bf16[256,256]{1,0:T(8,128)(2,1)} %modes_ref.1) | copy-start | bytes 393220

commit v6 on v5

--- a/solution.py
+++ b/solution.py
@@ -69,8 +69,8 @@
         pltpu.make_async_copy(taps_hbm, taps_ref, sems.at[2]),
         pltpu.make_async_copy(counters_hbm, counters_ref, sems.at[3]),
     ]
-    for copy in copies:
-        copy.start()
+    for k in (2, 0, 1, 3):
+        copies[k].start()
     copies[2].wait()
 
     @pl.when(jnp.logical_not(is_second()))

time: 51.4 us -> 51.2 us (level)
  no operation moved by 1% of the time
where the time goes in v6:
time: 51.2 us; the launch traced here: 51 us
  blocking collectives  39.9 us (78%)
  Pallas kernels  4.64 us (9%)
  starting transfers between devices  4.29 us (8%)
  waiting for transfers between devices  2.14 us (4%)
    all_to_all x1, blocking collectives, per_device(): parts = lax.all_to_all(partial, 'port', 0, 0, tiled=True)  21 us
    all_to_all x1, blocking collectives, per_device(): complete = lax.all_to_all(responses, 'port', 0, 0, tiled=True)  19 us
    ppermute x1, starting transfers between devices, per_device(): lax.ppermute(pair, 'tm', [(i, (i + 4) % steps) for i in range(steps)])  2.73 us
    pallas_call x1, Pallas kernels, per_device(): pl.pallas_call(merging_kernel, out_shape=(jax.ShapeDtypeStruct((ports, mo...  1.94 us
    ppermute x1, starting transfers between devices, per_device(): lax.ppermute(pair, 'tm', [(i, (i + 2) % steps) for i in range(steps)])  1.56 us
    ppermute x1, waiting for transfers between devices, per_device(): lax.ppermute(pair, 'tm', [(i, (i + 4) % steps) for i in range(steps)])  1.23 us
    pallas_call x1, Pallas kernels, per_device(): pl.pallas_call(sag_kernel, out_shape=jax.ShapeDtypeStruct((cycles, local_...  1.09 us
  transfers between devices with their start and end apart: 3, of which 2 were waited for; matrix products, arithmetic and copies ran while one was open for 0% of the time, Pallas kernels for 5%

profile of v6, /device:TPU:32, one launch (start us, length us, event | category | flops | bytes accessed | tf_op | source)
XLA Modules:
  0.0 51.0 jit_solution(1540836583260150476)
XLA Ops:
  0.0 0.0 copy-start.1
  0.0 0.0 collective-permute-start
  0.0 1.9 %shard_map.46 = (bf16[32,8,256]{2,1,0:T(8,128)(2,1)S(1)}, bf16[1024,256]{1,0:T(8,128)(2,1)S(1)}, bf16[256,4352]{1,0:T(8,128)(2,1)S(1)}) custom-call(bf16[256,256]{1,0:T(8,128)(2,1)} %signatures_hbm.1, bf16[256,256]{1,0:T(8,128)(2,1)} %modes_ref.1, bf16[1024,256]{1,0:T(8,128)(2,1)} %counters_hbm.1, bf16[8,4096]{1,0:T(8,128)(2,1)} %taps_ref.1), custom_call_target="tpu_custom_call" | custom-call | tf_op jit(solution)/shard_map/pallas_call | solution.py:238
  1.9 21.0 %all_to_all.10.parts_ref = bf16[32,8,256]{2,1,0:T(8,128)(2,1)S(1)} all-to-all(bf16[32,8,256]{2,1,0:T(8,128)(2,1)S(1)} %get-tuple-element.11), channel_id=1, replica_groups=mesh['tm'=8,'port'=32] {'port'}, dimensions={0} | all-to-all | bytes 262144 | tf_op jit(solution)/shard_map/all_to_all | solution.py:255
  22.9 0.0 collective-permute-done.other_ref
  22.9 0.4 shard_map.47.pair_ref
  23.3 1.6 %collective-permute-start.2 = (bf16[8,2048]{1,0:T(8,128)(2,1)S(1)}, bf16[8,2048]{1,0:T(8,128)(2,1)S(1)}, u32[]{:S(2)}, u32[]{:S(2)}) collective-permute-start(bf16[8,2048]{1,0:T(8,128)(2,1)S(1)} %shard_map.47.pair_ref), channel_id=1, source_target_pairs={{0,64},{32,96},{64,128},{96,160},{128,192},{160,224},{192,0},{224,... | collective-permute-start | bytes 98312 | tf_op jit(solution)/shard_map/ppermute | solution.py:259
  24.9 2.7 %collective-permute-start.1 = (bf16[8,2048]{1,0:T(8,128)(2,1)S(1)}, bf16[8,2048]{1,0:T(8,128)(2,1)S(1)}, u32[]{:S(2)}, u32[]{:S(2)}) collective-permute-start(bf16[8,2048]{1,0:T(8,128)(2,1)S(1)} %shard_map.47.pair_ref), channel_id=1, source_target_pairs={{0,128},{32,160},{64,192},{96,224},{128,0},{160,32},{192,64},{224,... | collective-permute-start | bytes 98312 | tf_op jit(solution)/shard_map/ppermute | solution.py:258
  27.6 0.9 %collective-permute-done.2.back1_ref = bf16[8,2048]{1,0:T(8,128)(2,1)S(1)} collective-permute-done((bf16[8,2048]{1,0:T(8,128)(2,1)S(1)}, bf16[8,2048]{1,0:T(8,128)(2,1)S(1)}, u32[]{:S(2)}, u32[]{:S(2)}) %collective-permute-start.2) | collective-permute-done | bytes 32800 | tf_op jit(solution)/shard_map/ppermute | solution.py:259
  28.5 0.0 copy-done.1
  28.5 0.5 %shard_map.48 = (f32[256,256]{1,0:T(8,128)S(1)}, bf16[34,32,128]{2,1,0:T(8,128)(2,1)S(1)}, bf16[256,4352]{1,0:T(8,128)(2,1)S(1)}) custom-call(bf16[8,2048]{1,0:T(8,128)(2,1)S(1)} %collective-permute-done.2.back1_ref, bf16[8,2048]{1,0:T(8,128)(2,1)S(1)} %shard_map.47.pair_ref, bf16[8,4096]{1,0:T(8,128)(2,1)S(1)} %copy-done.1, ...), custom_call_target="tpu_custom_call", output_to_operand_aliasing={{2}: (3, {})} | custom-call | flops 2000000000 | bytes 4456448 | tf_op jit(solution)/shard_map/pallas_call | solution.py:262
  29.0 0.0 copy-start
  29.0 1.2 %collective-permute-done.1.back2_ref = bf16[8,2048]{1,0:T(8,128)(2,1)S(1)} collective-permute-done((bf16[8,2048]{1,0:T(8,128)(2,1)S(1)}, bf16[8,2048]{1,0:T(8,128)(2,1)S(1)}, u32[]{:S(2)}, u32[]{:S(2)}) %collective-permute-start.1) | collective-permute-done | bytes 32800 | tf_op jit(solution)/shard_map/ppermute | solution.py:258
  30.3 0.7 %shard_map.49 = bf16[32,8,1024]{2,1,0:T(8,128)(2,1)S(1)} custom-call(bf16[8,2048]{1,0:T(8,128)(2,1)S(1)} %collective-permute-done.1.back2_ref, bf16[8,2048]{1,0:T(8,128)(2,1)S(1)} %collective-permute-done.2.back1_ref, f32[256,256]{1,0:T(8,128)S(1)} %get-tuple-element.14.near_ref, bf16[34,32,128]{2,1,0:T(8,128)(2,1)S(1)} %get-tuple-element.15.near_hankel_ref, ...), custom_call_target="tpu_custom_call" | custom-call | tf_op jit(solution)/shard_map/pallas_call | solution.py:273
  31.0 19.0 %all_to_all.11.responses_ref = bf16[32,8,1024]{2,1,0:T(8,128)(2,1)S(1)} all-to-all(bf16[32,8,1024]{2,1,0:T(8,128)(2,1)S(1)} %shard_map.49), channel_id=1, replica_groups=mesh['tm'=8,'port'=32] {'port'}, dimensions={0} | all-to-all | bytes 1048576 | tf_op jit(solution)/shard_map/all_to_all | solution.py:282
  49.9 0.0 copy-done
  49.9 1.1 %shard_map.50 = bf16[1024,256]{1,0:T(8,128)(2,1)} custom-call(bf16[32,8,1024]{2,1,0:T(8,128)(2,1)S(1)} %all_to_all.11.responses_ref, bf16[256,256]{1,0:T(8,128)(2,1)S(1)} %copy-done), custom_call_target="tpu_custom_call" | custom-call | tf_op jit(solution)/shard_map/pallas_call | solution.py:285
Async XLA Ops:
  0.0 28.5 %copy-start.1 = (bf16[8,4096]{1,0:T(8,128)(2,1)S(1)}, bf16[8,4096]{1,0:T(8,128)(2,1)}, u32[]{:S(2)}) copy-start(bf16[8,4096]{1,0:T(8,128)(2,1)} %taps_ref.1) | copy-start | bytes 196612
  0.0 22.9 %collective-permute-start = (bf16[1024,256]{1,0:T(8,128)(2,1)}, bf16[1024,256]{1,0:T(8,128)(2,1)S(1)}, u32[]{:S(2)}, u32[]{:S(2)}) collective-permute-start(bf16[1024,256]{1,0:T(8,128)(2,1)} %counters_hbm.1), channel_id=1, source_target_pairs={{0,32},{32,0},{64,96},{96,64},{128,160},{160,128},{192,224},{224,1... | collective-permute-start | bytes 1572872 | tf_op jit(solution)/shard_map/ppermute | solution.py:234
  23.3 5.2 %collective-permute-start.2 = (bf16[8,2048]{1,0:T(8,128)(2,1)S(1)}, bf16[8,2048]{1,0:T(8,128)(2,1)S(1)}, u32[]{:S(2)}, u32[]{:S(2)}) collective-permute-start(bf16[8,2048]{1,0:T(8,128)(2,1)S(1)} %shard_map.47.pair_ref), channel_id=1, source_target_pairs={{0,64},{32,96},{64,128},{96,160},{128,192},{160,224},{192,0},{224,... | collective-permute-start | bytes 98312 | tf_op jit(solution)/shard_map/ppermute | solution.py:259
  24.9 5.4 %collective-permute-start.1 = (bf16[8,2048]{1,0:T(8,128)(2,1)S(1)}, bf16[8,2048]{1,0:T(8,128)(2,1)S(1)}, u32[]{:S(2)}, u32[]{:S(2)}) collective-permute-start(bf16[8,2048]{1,0:T(8,128)(2,1)S(1)} %shard_map.47.pair_ref), channel_id=1, source_target_pairs={{0,128},{32,160},{64,192},{96,224},{128,0},{160,32},{192,64},{224,... | collective-permute-start | bytes 98312 | tf_op jit(solution)/shard_map/ppermute | solution.py:258
  29.0 20.9 %copy-start = (bf16[256,256]{1,0:T(8,128)(2,1)S(1)}, bf16[256,256]{1,0:T(8,128)(2,1)}, u32[]{:S(2)}) copy-start(bf16[256,256]{1,0:T(8,128)(2,1)} %modes_ref.1) | copy-start | bytes 393220

commit v7 on v5

--- a/solution.py
+++ b/solution.py
@@ -71,18 +71,18 @@
     ]
     for copy in copies:
         copy.start()
-    copies[2].wait()
-
-    @pl.when(jnp.logical_not(is_second()))
-    def _():
-        fill_toeplitz(taps_ref.shape[1] // LANES, toeplitz_ref.shape[1], taps_ref, toeplitz_ref)
-
     copies[0].wait()
     copies[1].wait()
     partial = lax.dot_general(
         modes_ref[...], signatures_ref[...], (((0,), (1,)), ((), ())), preferred_element_type=jnp.float32
     )
     partial_ref[...] = partial.reshape(partial_ref.shape).astype(partial_ref.dtype)
+
+    copies[2].wait()
+
+    @pl.when(jnp.logical_not(is_second()))
+    def _():
+        fill_toeplitz(taps_ref.shape[1] // LANES, toeplitz_ref.shape[1], taps_ref, toeplitz_ref)
 
     copies[3].wait()
 

time: 51.4 us -> 51.4 us (level)
  no operation moved by 1% of the time
where the time goes in v7:
time: 51.4 us; the launch traced here: 51.2 us
  blocking collectives  40 us (78%)
  Pallas kernels  4.74 us (9%)
  starting transfers between devices  4.29 us (8%)
  waiting for transfers between devices  2.14 us (4%)
    all_to_all x1, blocking collectives, per_device(): parts = lax.all_to_all(partial, 'port', 0, 0, tiled=True)  20.9 us
    all_to_all x1, blocking collectives, per_device(): complete = lax.all_to_all(responses, 'port', 0, 0, tiled=True)  19.1 us
    ppermute x1, starting transfers between devices, per_device(): lax.ppermute(pair, 'tm', [(i, (i + 4) % steps) for i in range(steps)])  2.73 us
    pallas_call x1, Pallas kernels, per_device(): pl.pallas_call(merging_kernel, out_shape=(jax.ShapeDtypeStruct((ports, mo...  2.03 us
    ppermute x1, starting transfers between devices, per_device(): lax.ppermute(pair, 'tm', [(i, (i + 2) % steps) for i in range(steps)])  1.56 us
    ppermute x1, waiting for transfers between devices, per_device(): lax.ppermute(pair, 'tm', [(i, (i + 4) % steps) for i in range(steps)])  1.23 us
    pallas_call x1, Pallas kernels, per_device(): pl.pallas_call(sag_kernel, out_shape=jax.ShapeDtypeStruct((cycles, local_...  1.09 us
  transfers between devices with their start and end apart: 3, of which 2 were waited for; matrix products, arithmetic and copies ran while one was open for 0% of the time, Pallas kernels for 5%

profile of v7, /device:TPU:32, one launch (start us, length us, event | category | flops | bytes accessed | tf_op | source)
XLA Modules:
  0.0 51.2 jit_solution(301016972036876401)
XLA Ops:
  0.0 0.0 copy-start.1
  0.0 0.0 collective-permute-start
  0.0 2.0 %shard_map.46 = (bf16[32,8,256]{2,1,0:T(8,128)(2,1)S(1)}, bf16[1024,256]{1,0:T(8,128)(2,1)S(1)}, bf16[256,4352]{1,0:T(8,128)(2,1)S(1)}) custom-call(bf16[256,256]{1,0:T(8,128)(2,1)} %signatures_hbm.1, bf16[256,256]{1,0:T(8,128)(2,1)} %modes_ref.1, bf16[1024,256]{1,0:T(8,128)(2,1)} %counters_hbm.1, bf16[8,4096]{1,0:T(8,128)(2,1)} %taps_ref.1), custom_call_target="tpu_custom_call" | custom-call | tf_op jit(solution)/shard_map/pallas_call | solution.py:238
  2.0 20.9 %all_to_all.10.parts_ref = bf16[32,8,256]{2,1,0:T(8,128)(2,1)S(1)} all-to-all(bf16[32,8,256]{2,1,0:T(8,128)(2,1)S(1)} %get-tuple-element.11), channel_id=1, replica_groups=mesh['tm'=8,'port'=32] {'port'}, dimensions={0} | all-to-all | bytes 262144 | tf_op jit(solution)/shard_map/all_to_all | solution.py:255
  22.9 0.0 collective-permute-done.other_ref
  22.9 0.4 shard_map.47.pair_ref
  23.3 1.6 %collective-permute-start.2 = (bf16[8,2048]{1,0:T(8,128)(2,1)S(1)}, bf16[8,2048]{1,0:T(8,128)(2,1)S(1)}, u32[]{:S(2)}, u32[]{:S(2)}) collective-permute-start(bf16[8,2048]{1,0:T(8,128)(2,1)S(1)} %shard_map.47.pair_ref), channel_id=1, source_target_pairs={{0,64},{32,96},{64,128},{96,160},{128,192},{160,224},{192,0},{224,... | collective-permute-start | bytes 98312 | tf_op jit(solution)/shard_map/ppermute | solution.py:259
  24.9 2.7 %collective-permute-start.1 = (bf16[8,2048]{1,0:T(8,128)(2,1)S(1)}, bf16[8,2048]{1,0:T(8,128)(2,1)S(1)}, u32[]{:S(2)}, u32[]{:S(2)}) collective-permute-start(bf16[8,2048]{1,0:T(8,128)(2,1)S(1)} %shard_map.47.pair_ref), channel_id=1, source_target_pairs={{0,128},{32,160},{64,192},{96,224},{128,0},{160,32},{192,64},{224,... | collective-permute-start | bytes 98312 | tf_op jit(solution)/shard_map/ppermute | solution.py:258
  27.6 0.9 %collective-permute-done.2.back1_ref = bf16[8,2048]{1,0:T(8,128)(2,1)S(1)} collective-permute-done((bf16[8,2048]{1,0:T(8,128)(2,1)S(1)}, bf16[8,2048]{1,0:T(8,128)(2,1)S(1)}, u32[]{:S(2)}, u32[]{:S(2)}) %collective-permute-start.2) | collective-permute-done | bytes 32800 | tf_op jit(solution)/shard_map/ppermute | solution.py:259
  28.5 0.0 copy-done.1
  28.5 0.5 %shard_map.48 = (f32[256,256]{1,0:T(8,128)S(1)}, bf16[34,32,128]{2,1,0:T(8,128)(2,1)S(1)}, bf16[256,4352]{1,0:T(8,128)(2,1)S(1)}) custom-call(bf16[8,2048]{1,0:T(8,128)(2,1)S(1)} %collective-permute-done.2.back1_ref, bf16[8,2048]{1,0:T(8,128)(2,1)S(1)} %shard_map.47.pair_ref, bf16[8,4096]{1,0:T(8,128)(2,1)S(1)} %copy-done.1, ...), custom_call_target="tpu_custom_call", output_to_operand_aliasing={{2}: (3, {})} | custom-call | flops 2000000000 | bytes 4456448 | tf_op jit(solution)/shard_map/pallas_call | solution.py:262
  29.0 0.0 copy-start
  29.1 1.2 %collective-permute-done.1.back2_ref = bf16[8,2048]{1,0:T(8,128)(2,1)S(1)} collective-permute-done((bf16[8,2048]{1,0:T(8,128)(2,1)S(1)}, bf16[8,2048]{1,0:T(8,128)(2,1)S(1)}, u32[]{:S(2)}, u32[]{:S(2)}) %collective-permute-start.1) | collective-permute-done | bytes 32800 | tf_op jit(solution)/shard_map/ppermute | solution.py:258
  30.3 0.7 %shard_map.49 = bf16[32,8,1024]{2,1,0:T(8,128)(2,1)S(1)} custom-call(bf16[8,2048]{1,0:T(8,128)(2,1)S(1)} %collective-permute-done.1.back2_ref, bf16[8,2048]{1,0:T(8,128)(2,1)S(1)} %collective-permute-done.2.back1_ref, f32[256,256]{1,0:T(8,128)S(1)} %get-tuple-element.14.near_ref, bf16[34,32,128]{2,1,0:T(8,128)(2,1)S(1)} %get-tuple-element.15.near_hankel_ref, ...), custom_call_target="tpu_custom_call" | custom-call | tf_op jit(solution)/shard_map/pallas_call | solution.py:273
  31.0 19.1 %all_to_all.11.responses_ref = bf16[32,8,1024]{2,1,0:T(8,128)(2,1)S(1)} all-to-all(bf16[32,8,1024]{2,1,0:T(8,128)(2,1)S(1)} %shard_map.49), channel_id=1, replica_groups=mesh['tm'=8,'port'=32] {'port'}, dimensions={0} | all-to-all | bytes 1048576 | tf_op jit(solution)/shard_map/all_to_all | solution.py:282
  50.1 0.0 copy-done
  50.1 1.1 %shard_map.50 = bf16[1024,256]{1,0:T(8,128)(2,1)} custom-call(bf16[32,8,1024]{2,1,0:T(8,128)(2,1)S(1)} %all_to_all.11.responses_ref, bf16[256,256]{1,0:T(8,128)(2,1)S(1)} %copy-done), custom_call_target="tpu_custom_call" | custom-call | tf_op jit(solution)/shard_map/pallas_call | solution.py:285
Async XLA Ops:
  0.0 28.5 %copy-start.1 = (bf16[8,4096]{1,0:T(8,128)(2,1)S(1)}, bf16[8,4096]{1,0:T(8,128)(2,1)}, u32[]{:S(2)}) copy-start(bf16[8,4096]{1,0:T(8,128)(2,1)} %taps_ref.1) | copy-start | bytes 196612
  0.0 22.9 %collective-permute-start = (bf16[1024,256]{1,0:T(8,128)(2,1)}, bf16[1024,256]{1,0:T(8,128)(2,1)S(1)}, u32[]{:S(2)}, u32[]{:S(2)}) collective-permute-start(bf16[1024,256]{1,0:T(8,128)(2,1)} %counters_hbm.1), channel_id=1, source_target_pairs={{0,32},{32,0},{64,96},{96,64},{128,160},{160,128},{192,224},{224,1... | collective-permute-start | bytes 1572872 | tf_op jit(solution)/shard_map/ppermute | solution.py:234
  23.3 5.2 %collective-permute-start.2 = (bf16[8,2048]{1,0:T(8,128)(2,1)S(1)}, bf16[8,2048]{1,0:T(8,128)(2,1)S(1)}, u32[]{:S(2)}, u32[]{:S(2)}) collective-permute-start(bf16[8,2048]{1,0:T(8,128)(2,1)S(1)} %shard_map.47.pair_ref), channel_id=1, source_target_pairs={{0,64},{32,96},{64,128},{96,160},{128,192},{160,224},{192,0},{224,... | collective-permute-start | bytes 98312 | tf_op jit(solution)/shard_map/ppermute | solution.py:259
  24.9 5.4 %collective-permute-start.1 = (bf16[8,2048]{1,0:T(8,128)(2,1)S(1)}, bf16[8,2048]{1,0:T(8,128)(2,1)S(1)}, u32[]{:S(2)}, u32[]{:S(2)}) collective-permute-start(bf16[8,2048]{1,0:T(8,128)(2,1)S(1)} %shard_map.47.pair_ref), channel_id=1, source_target_pairs={{0,128},{32,160},{64,192},{96,224},{128,0},{160,32},{192,64},{224,... | collective-permute-start | bytes 98312 | tf_op jit(solution)/shard_map/ppermute | solution.py:258
  29.0 21.0 %copy-start = (bf16[256,256]{1,0:T(8,128)(2,1)S(1)}, bf16[256,256]{1,0:T(8,128)(2,1)}, u32[]{:S(2)}) copy-start(bf16[256,256]{1,0:T(8,128)(2,1)} %modes_ref.1) | copy-start | bytes 393220
